TPU v7x, 32 devices: a whole 2x2x4 slice. The times are simulated.
32 devices in a mesh: wide: 4 (over y, x), narrow: 8 (over z, core).
Axes of the slice: x: 2, y: 2, z: 4, core: 2. Of those that a mesh axis runs over, the one named last changes fastest.
Arguments:
- volume_field: float32 [2, 8, 64, 128, 512], P(None, None, 'wide', 'narrow'), may hold values from -6 to 6
- coefficients: bfloat16 [3, 64, 128, 512], P(None, 'wide', 'narrow'), may hold values from 0.25 to 1
- density: float32 [2, 8, 65536], P(None, None, 'narrow'), may hold values from -6 to 6
- boundary_matrix: bfloat16 [2, 4, 256, 65536], P(None, None, 'wide', 'narrow'), may hold values from -0.03125 to 0.03125
- upsample: int32 [128], P('narrow'), may hold values from 1 to 4, as said below
- trace_cell: int32 [4, 8, 256], P('wide', 'narrow'), may hold values from 0 to 255
- trace_row: int32 [4, 8, 256], P('wide', 'narrow'), may hold values from 0 to 255, as said below
- slot_counts: int32 [4, 8], P('wide', 'narrow'), may hold values from 192 to 256, as said below
Outputs:
- volume_out: float32 [2, 8, 64, 128, 512], P(None, None, 'wide', 'narrow')
- boundary_out: float32 [2, 8, 256], P(None, None, ('wide', 'narrow'))
Inputs may be any that keep to these rules, and one draw needn't show every extreme that they name: `trace_row`: live slots of one brick name rows of one owner (rows k * 8 to (k + 1) * 8 - 1) at most 16 times; in every draw one owner is named 16 times by the live slots of every brick. `slot_counts`: some brick has all 256 slots live. `upsample`: some panel group has factor 4 and some has factor 1.
All inputs are finite; a program needn't handle non-finite values.
Results may differ from a plain program's by a relative error of at most 0.0019.
Values sent between devices are 32-bit elements; how exact they have to be, the bound alone decides.
A program may use at most 192 MiB of HBM per device.

v0:
```python
from functools import partial

import jax
import jax.numpy as jnp
from jax import lax
from jax.sharding import PartitionSpec as P

UMAX = 4


def extended(value, sides, width):
    for axis, dim in sides:
        peers, length = (lax.axis_size(axis), value.shape[dim])
        up = [(i, (i + 1) % peers) for i in range(peers - 1)]
        down = [(j, i) for i, j in up]
        last = lax.slice_in_dim(value, length - width, length, axis=dim)
        first = lax.slice_in_dim(value, 0, width, axis=dim)
        before = lax.ppermute(last, axis, up)
        after = lax.ppermute(first, axis, down)
        value = jnp.concatenate([before, value, after], axis=dim)
    return value


def stencil_apply(padded, volume, coefficients):
    size_x, size_y, size_z = (volume.shape[2], volume.shape[3], volume.shape[4])
    widened = jnp.pad(padded, ((0, 0), (0, 0), (0, 0), (0, 0), (1, 1)))
    edge_sum = jnp.zeros(volume.shape, jnp.float32)
    corner_sum = jnp.zeros(volume.shape, jnp.float32)
    for across in (-1, 0, 1):
        for along in (-1, 0, 1):
            for upward in (-1, 0, 1):
                moved = abs(across) + abs(along) + abs(upward)
                if moved < 2:
                    continue
                shifted = widened[
                    :,
                    :,
                    1 + across : 1 + across + size_x,
                    1 + along : 1 + along + size_y,
                    1 + upward : 1 + upward + size_z,
                ]
                if moved == 2:
                    edge_sum = edge_sum + shifted
                else:
                    corner_sum = corner_sum + shifted
    stiffness = 8.0 / 3.0 * volume - edge_sum / 6.0 - corner_sum / 12.0
    scales = coefficients.astype(jnp.float32)
    turned = jnp.stack([volume[1], -volume[0]])
    return scales[0] * stiffness - scales[1] * volume + scales[2] * turned


def level_product(level_index, blocks_density, following, factor, upsample, boundary_matrix):
    blend = level_index / factor
    fine = jnp.where(
        level_index < upsample[None, :, None],
        ((1.0 - blend) * blocks_density + blend * following) / factor,
        0.0,
    )
    fine = fine.reshape(blocks_density.shape[0], -1).astype(jnp.bfloat16)
    matrix = boundary_matrix[:, level_index]
    matrix = matrix.reshape(2 * matrix.shape[1], matrix.shape[2])
    return lax.dot_general(
        matrix, fine, (((1,), (1,)), ((), ())), preferred_element_type=jnp.float32
    )


def on_device(
    volume_field,
    coefficients,
    density,
    boundary_matrix,
    upsample,
    trace_cell,
    trace_row,
    slot_counts,
):
    padded = extended(volume_field, (("wide", 2), ("narrow", 3)), 1)
    operated = stencil_apply(padded, volume_field, coefficients)
    waves = volume_field.shape[1]
    group_rows = boundary_matrix.shape[2]
    block_count = upsample.shape[0]
    blocks_density = density.reshape(2 * waves, block_count, -1)
    following = jnp.concatenate([blocks_density[:, :, 1:], blocks_density[:, :, -1:]], axis=2)
    factor = upsample.astype(jnp.float32)[None, :, None]
    highest = jnp.max(upsample)
    products = level_product(0, blocks_density, following, factor, upsample, boundary_matrix)

    def nothing_done():
        return jnp.zeros((2 * group_rows, 2 * waves), jnp.float32)

    for level_index in range(1, UMAX):
        products = products + lax.cond(
            level_index < highest,
            partial(
                level_product,
                level_index,
                blocks_density,
                following,
                factor,
                upsample,
                boundary_matrix,
            ),
            nothing_done,
        )
    real_rows = products[:group_rows, :waves] - products[group_rows:, waves:]
    imag_rows = products[:group_rows, waves:] + products[group_rows:, :waves]
    partial_rows = jnp.concatenate([real_rows, imag_rows], axis=1)
    rows_each = group_rows // lax.axis_size("narrow")
    whole_rows = lax.psum(partial_rows, "narrow")
    own_rows = lax.dynamic_slice_in_dim(
        whole_rows, lax.axis_index("narrow") * rows_each, rows_each, 0
    )
    device_count = lax.axis_size("wide") * lax.axis_size("narrow")
    slot_total = trace_row.shape[2]
    capacity = max(2, 2 * slot_total // device_count)
    size_x, size_y = (volume_field.shape[2], volume_field.shape[3])
    slot_rows = trace_row.reshape(slot_total)
    slot_cells = trace_cell.reshape(slot_total)
    live_count = slot_counts.reshape(())
    slot_index = jnp.arange(slot_total, dtype=jnp.int32)
    live_mask = slot_index < live_count
    picker = (slot_cells[None, :] == jnp.arange(size_x * size_y, dtype=jnp.int32)[:, None]).astype(
        jnp.float32
    )
    top_plane = volume_field[:, :, :, :, -1].reshape(2 * waves, size_x * size_y)
    slot_values = jnp.dot(top_plane, picker, precision=lax.Precision.HIGHEST)
    owners = slot_rows // rows_each
    local_row = slot_rows % rows_each
    owner_hits = (
        (owners[:, None] == jnp.arange(device_count, dtype=jnp.int32)[None, :]) & live_mask[:, None]
    ).astype(jnp.int32)
    earlier = jnp.cumsum(owner_hits, axis=0) - owner_hits
    slot_rank = jnp.sum(earlier * owner_hits, axis=1)
    target = jnp.where(live_mask, owners * capacity + slot_rank, -1)
    buffer_index = jnp.arange(device_count * capacity, dtype=jnp.int32)
    placing_mask = target[None, :] == buffer_index[:, None]
    placing = placing_mask.astype(jnp.float32)
    outgoing = lax.dot_general(
        placing, slot_values, (((1,), (1,)), ((), ())), precision=lax.Precision.HIGHEST
    )
    send_rows = jnp.sum(jnp.where(placing_mask, local_row[None, :] + 1, 0), axis=1) - 1
    arrived, arrived_rows = (
        lax.all_to_all(outgoing, ("wide", "narrow"), split_axis=0, concat_axis=0, tiled=True),
        lax.all_to_all(send_rows, ("wide", "narrow"), split_axis=0, concat_axis=0, tiled=True),
    )
    row_hit = (arrived_rows[None, :] == jnp.arange(rows_each, dtype=jnp.int32)[:, None]).astype(
        jnp.float32
    )
    trace_sum = jnp.dot(row_hit, arrived, precision=lax.Precision.HIGHEST)
    boundary_out = (own_rows - 0.25 * trace_sum).T.reshape(2, waves, rows_each)
    answers = lax.dot_general(
        row_hit, own_rows, (((0,), (0,)), ((), ())), precision=lax.Precision.HIGHEST
    )
    returned = lax.all_to_all(answers, ("wide", "narrow"), split_axis=0, concat_axis=0, tiled=True)
    slot_back = lax.dot_general(
        placing, returned, (((0,), (0,)), ((), ())), precision=lax.Precision.HIGHEST
    )
    cell_add = jnp.dot(picker, slot_back, precision=lax.Precision.HIGHEST)
    cell_add = cell_add.T.reshape(2, waves, size_x, size_y)
    volume_out = operated.at[:, :, :, :, -1].add(cell_add)
    return (volume_out, boundary_out)


def solution(mesh):
    return jax.shard_map(
        on_device,
        mesh=mesh,
        in_specs=(
            P(None, None, "wide", "narrow", None),
            P(None, "wide", "narrow", None),
            P(None, None, "narrow"),
            P(None, None, "wide", "narrow"),
            P("narrow"),
            P("wide", "narrow", None),
            P("wide", "narrow", None),
            P("wide", "narrow"),
        ),
        out_specs=(P(None, None, "wide", "narrow", None), P(None, None, ("wide", "narrow"))),
        check_vma=False,
    )
```

profile of v0, /device:TPU:1, one launch (start us, length us, event | category | flops | bytes accessed | tf_op | source)
XLA Modules:
  0.0 275.6 jit_solution(2263501250669316070)
XLA Ops:
  0.7 11.0 %copy.37 = f32[2,8,16,16,512]{4,1,3,2,0:T(8,128)S(1)} copy(f32[2,8,16,16,512]{4,3,2,1,0:T(8,128)} %param.16) | data formatting | bytes 16777216 | tf_op args[0]
  11.7 3.4 %copy-done.1 = f32[2,8,16,16,512]{4,1,3,2,0:T(8,128)} copy-done((f32[2,8,16,16,512]{4,1,3,2,0:T(8,128)}, f32[2,8,16,16,512]{4,1,3,2,0:T(8,128)S(1)}, u32[]{:S(2)}) %copy-start.1) | copy-done | bytes 8388632
  16.2 4.7 %collective-permute-start = (f32[2,8,1,16,512]{4,1,3,2,0:T(8,128)}, f32[2,8,1,16,512]{4,1,3,2,0:T(8,128)}, u32[]{:S(2)}, u32[]{:S(2)}) collective-permute-start(f32[2,8,1,16,512]{4,1,3,2,0:T(8,128)} %get-tuple-element.89), channel_id=1, source_target_pairs={{0,8},{8,16},{16,24},{1,9},{9,17},{17,25},{2,10},{10,18},{18,26},{... | collective-permute-start | bytes 1572872 | tf_op jit(solution)/shard_map/ppermute | solution.py:18
  24.7 7.7 %all-to-all-start = ((s32[32,16,1]{1,2,0:T(1,128)}), s32[32,16,1]{1,2,0:T(1,128)S(1)}, u32[]{:S(2)}, u32[]{:S(2)}) async-start(s32[32,16,1]{1,2,0:T(1,128)} %bitcast.22), calls=%async_computation | async-start | bytes 32768 | tf_op jit(solution)/shard_map/all_to_all | solution.py:144
  34.5 2.8 %slice_reduce_fusion = f32[2,8,16,16]{3,2,1,0:T(8,128)S(1)} fusion(f32[2,8,16,16,512]{4,3,2,1,0:T(8,128)} %param.16), kind=kLoop, calls=%fused_computation.56 | loop fusion | bytes 32768 | tf_op jit(solution)/shard_map/slice | solution.py:125
  44.7 13.4 %conditional.5 = (f32[128,16]{0,1:T(8,128)S(1)}) conditional(s32[]{:T(128)} %convert_element_type.59, () %tuple.33, (s32[16]{0:T(128)S(1)}, f32[1,16,1]{1,2,0:T(1,128)S(1)}, f32[16,16,512]{2,1,0:T(8,128)S(1)}, f32[16,16,512]{2,1,0:T(8,128)S(1)}, bf16[2,4,64,8192]{3,2,1,0:T(8,128)(2,1)}) %tuple.62), branch_computations={%region_9.10_spmd, %region_10.11_spmd} | conditional | flops 34340912 | bytes 8397288 | solution.py:92
  55.7 1.7 slice.125
  58.1 2.8 %conditional.4 = (f32[128,16]{0,1:T(8,128)S(1)}) conditional(s32[]{:T(128)} %convert_element_type.58, () %tuple.32, (s32[16]{0:T(128)S(1)}, f32[1,16,1]{1,2,0:T(1,128)S(1)}, f32[16,16,512]{2,1,0:T(8,128)S(1)}, f32[16,16,512]{2,1,0:T(8,128)S(1)}, bf16[2,4,64,8192]{3,2,1,0:T(8,128)(2,1)}) %tuple.63), branch_computations={%region_7.8_spmd, %region_8.9_spmd} | conditional | flops 34340912 | bytes 8397288 | solution.py:92
  60.9 2.8 %conditional.3 = (f32[128,16]{0,1:T(8,128)S(1)}) conditional(s32[]{:T(128)} %convert_element_type.57, () %tuple.30, (s32[16]{0:T(128)S(1)}, f32[1,16,1]{1,2,0:T(1,128)S(1)}, f32[16,16,512]{2,1,0:T(8,128)S(1)}, f32[16,16,512]{2,1,0:T(8,128)S(1)}, bf16[2,4,64,8192]{3,2,1,0:T(8,128)(2,1)}) %tuple.64), branch_computations={%region_5.6_spmd, %region_6.7_spmd} | conditional | flops 34340912 | bytes 8397288 | solution.py:92
  63.7 1.9 fusion.25
  67.3 8.4 %fusion.53 = (f32[1,8,16,16,512]{4,1,3,2,0:T(8,128)}, f32[1,8,16,16,512]{4,1,3,2,0:T(8,128)}) fusion(f32[2,8,16,16,512]{4,1,3,2,0:T(8,128)} %copy-done.1), kind=kLoop, calls=%fused_computation.134 | loop fusion | flops 1048576 | bytes 16777216 | tf_op jit(solution)/shard_map/slice | solution.py:48
  75.7 11.1 %psum.7 = f32[64,16]{0,1:T(8,128)S(1)} all-reduce(f32[64,16]{0,1:T(8,128)S(1)} %pad_maximum_fusion.3), channel_id=1, replica_groups=mesh['wide'=4,'narrow'=8] {'narrow'}, use_global_device_ids=true, to_apply=%region_11.12 | all-reduce | flops 1024 | bytes 8192 | tf_op jit(solution)/shard_map/psum | solution.py:109
  86.8 5.9 %all-to-all-start.2 = ((f32[32,1,256]{2,1,0:T(1,128)}), f32[32,1,256]{2,1,0:T(1,128)S(1)}, u32[]{:S(2)}, u32[]{:S(2)}) async-start(f32[32,1,256]{2,1,0:T(1,128)} %reshape.271), calls=%async_computation.2 | async-start | bytes 65536 | tf_op jit(solution)/shard_map/all_to_all | solution.py:143
  95.1 12.5 %constant_dynamic-update-slice_fusion.1 = f32[2,8,18,16,512]{4,1,3,2,0:T(8,128)S(1)} fusion(f32[2,8,18,16,512]{4,1,3,2,0:T(8,128)S(1)} %constant_dynamic-update-slice_fusion.2, f32[2,8,16,16,512]{4,3,2,1,0:T(8,128)} %param.16), kind=kLoop, calls=%fused_computation.103 | loop fusion | bytes 16777216
  108.7 3.6 %copy-done = f32[2,8,18,16,512]{4,1,3,2,0:T(8,128)} copy-done((f32[2,8,18,16,512]{4,1,3,2,0:T(8,128)}, f32[2,8,18,16,512]{4,1,3,2,0:T(8,128)S(1)}, u32[]{:S(2)}) %copy-start) | copy-done | bytes 9437208
  113.4 2.2 collective-permute-start.3
  115.6 3.4 %collective-permute-start.2 = (f32[2,8,18,1,512]{4,1,3,2,0:T(8,128)}, f32[2,8,18,1,512]{4,1,3,2,0:T(8,128)S(1)}, u32[]{:S(2)}, u32[]{:S(2)}) collective-permute-start(f32[2,8,18,1,512]{4,1,3,2,0:T(8,128)} %get-tuple-element.84), channel_id=1, source_target_pairs={{0,1},{1,2},{2,3},{3,4},{4,5},{5,6},{6,7},{8,9},{9,10},{10,11},{11... | collective-permute-start | bytes 1769480 | tf_op jit(solution)/shard_map/ppermute | solution.py:18
  120.2 4.6 %all-to-all-start.1 = ((f32[32,1,256]{2,1,0:T(1,128)}), f32[32,1,256]{2,1,0:T(1,128)S(1)}, u32[]{:S(2)}, u32[]{:S(2)}) async-start(f32[32,1,256]{2,1,0:T(1,128)} %reshape.269), calls=%async_computation.1 | async-start | bytes 65536 | tf_op jit(solution)/shard_map/all_to_all | solution.py:154
  127.3 4.7 %all-to-all-done.1 = f32[32,1,256]{2,1,0:T(1,128)S(1)} async-done(((f32[32,1,256]{2,1,0:T(1,128)}), f32[32,1,256]{2,1,0:T(1,128)S(1)}, u32[]{:S(2)}, u32[]{:S(2)}) %all-to-all-start.1) | async-done | bytes 32800 | tf_op jit(solution)/shard_map/all_to_all | solution.py:154
  135.3 11.8 %select_maximum_fusion = f32[2,8,18,18,514]{4,1,3,2,0:T(8,128)} fusion(f32[2,8,18,1,512]{4,1,3,2,0:T(8,128)S(1)} %collective-permute-done.3, f32[2,8,18,16,512]{4,1,3,2,0:T(8,128)} %copy-done, f32[2,8,18,1,512]{4,1,3,2,0:T(8,128)S(1)} %collective-permute-done.2), kind=kLoop, calls=%fused_computation.17 | loop fusion | flops 21316608 | bytes 21275136 | tf_op jit(solution)/shard_map/concatenate | solution.py:20
  147.1 70.4 %fusion.16 = f32[2,8,16,16,512]{4,1,3,2,0:T(8,128)} fusion(f32[2,8,18,16,512]{4,1,3,2,0:T(8,128)} %copy-done, f32[2,8,18,1,512]{4,1,3,2,0:T(8,128)S(1)} %collective-permute-done.3, f32[2,8,18,1,512]{4,1,3,2,0:T(8,128)S(1)} %collective-permute-done.2, f32[2,8,18,18,514]{4,1,3,2,0:T(8,128)} %select_maximum_fusion, ...), kind=kLoop, calls=%fused_computation.39 | loop fusion | flops 69206016 | bytes 171573248 | tf_op jit(solution)/shard_map/add | solution.py:49
  217.5 3.5 %slice_add_fusion.7 = f32[2,8,16,16,1]{4,1,3,2,0:T(8,128)} fusion(f32[2,8,16,16,1]{4,1,3,2,0:T(8,128)S(1)} %copy.48, f32[2,8,16,16,512]{4,1,3,2,0:T(8,128)} %fusion.16), kind=kLoop, calls=%fused_computation.55 | loop fusion | flops 4096 | bytes 49152 | tf_op jit(solution)/shard_map/add | solution.py:160
  221.0 42.6 %scatter-add.4 = f32[2,8,16,16,512]{4,1,3,2,0:T(8,128)} dynamic-update-slice(f32[2,8,16,16,512]{4,1,3,2,0:T(8,128)} %fusion.16, f32[2,8,16,16,1]{4,1,3,2,0:T(8,128)} %slice_add_fusion.7, s32[]{:T(128)} %constant.112.clone.1, s32[]{:T(128)} %constant.112.clone.1, s32[]{:T(128)} %constant.112.clone.1, s32[]{:T(128)} %constant.112.clone.1, s32[]{:T(128)} %constant.124.clone.1) | dynamic-update-slice | bytes 32772 | tf_op jit(solution)/shard_map/scatter-add | solution.py:160
  263.6 11.6 %copy.53 = f32[2,8,16,16,512]{4,3,2,1,0:T(8,128)} copy(f32[2,8,16,16,512]{4,1,3,2,0:T(8,128)} %scatter-add.4) | data formatting | bytes 16777216
  (101 shorter events, 31.3 us)
Async XLA Ops:
  0.6 21.6 %copy-start.4 = (s32[1,1,256]{2,1,0:T(1,128)S(1)}, s32[1,1,256]{2,1,0:T(1,128)}, u32[]{:S(2)}) copy-start(s32[1,1,256]{2,1,0:T(1,128)} %param.22) | copy-start | bytes 3076
  0.6 31.8 %copy-start.3 = (f32[2,8,8192]{2,1,0:T(8,128)S(1)}, f32[2,8,8192]{2,1,0:T(8,128)}, u32[]{:S(2)}) copy-start(f32[2,8,8192]{2,1,0:T(8,128)} %param.18) | copy-start | bytes 1572868
  0.7 33.2 %copy-start.5 = (s32[16]{0:T(128)S(1)}, s32[16]{0:T(128)}, u32[]{:S(2)}) copy-start(s32[16]{0:T(128)} %param.20) | copy-start | bytes 196
  0.7 36.6 %copy-start.2 = (bf16[3,16,16,512]{3,2,1,0:T(8,128)(2,1)S(1)}, bf16[3,16,16,512]{3,2,1,0:T(8,128)(2,1)}, u32[]{:S(2)}) copy-start(bf16[3,16,16,512]{3,2,1,0:T(8,128)(2,1)} %param.17) | copy-start | bytes 2359300
  11.7 3.4 %copy-start.1 = (f32[2,8,16,16,512]{4,1,3,2,0:T(8,128)}, f32[2,8,16,16,512]{4,1,3,2,0:T(8,128)S(1)}, u32[]{:S(2)}) copy-start(f32[2,8,16,16,512]{4,1,3,2,0:T(8,128)S(1)} %copy.37) | copy-start | bytes 25165828
  16.2 77.9 %collective-permute-start = (f32[2,8,1,16,512]{4,1,3,2,0:T(8,128)}, f32[2,8,1,16,512]{4,1,3,2,0:T(8,128)}, u32[]{:S(2)}, u32[]{:S(2)}) collective-permute-start(f32[2,8,1,16,512]{4,1,3,2,0:T(8,128)} %get-tuple-element.89), channel_id=1, source_target_pairs={{0,8},{8,16},{16,24},{1,9},{9,17},{17,25},{2,10},{10,18},{18,26},{... | collective-permute-start | bytes 1572872 | tf_op jit(solution)/shard_map/ppermute | solution.py:18
  20.9 86.7 %collective-permute-start.1 = (f32[2,8,1,16,512]{4,1,3,2,0:T(8,128)}, f32[2,8,1,16,512]{4,1,3,2,0:T(8,128)}, u32[]{:S(2)}, u32[]{:S(2)}) collective-permute-start(f32[2,8,1,16,512]{4,1,3,2,0:T(8,128)} %get-tuple-element.88), channel_id=1, source_target_pairs={{8,0},{16,8},{24,16},{9,1},{17,9},{25,17},{10,2},{18,10},{26,18},{... | collective-permute-start | bytes 1572872 | tf_op jit(solution)/shard_map/ppermute | solution.py:19
  24.7 62.1 %all-to-all-start = ((s32[32,16,1]{1,2,0:T(1,128)}), s32[32,16,1]{1,2,0:T(1,128)S(1)}, u32[]{:S(2)}, u32[]{:S(2)}) async-start(s32[32,16,1]{1,2,0:T(1,128)} %bitcast.22), calls=%async_computation | async-start | bytes 32768 | tf_op jit(solution)/shard_map/all_to_all | solution.py:144
  58.1 7.6 %copy-start.6 = (s32[1,1,256]{2,1,0:T(1,128)S(1)}, s32[1,1,256]{2,1,0:T(1,128)}, u32[]{:S(2)}) copy-start(s32[1,1,256]{2,1,0:T(1,128)} %param.21) | copy-start | bytes 3076
  86.8 33.4 %all-to-all-start.2 = ((f32[32,1,256]{2,1,0:T(1,128)}), f32[32,1,256]{2,1,0:T(1,128)S(1)}, u32[]{:S(2)}, u32[]{:S(2)}) async-start(f32[32,1,256]{2,1,0:T(1,128)} %reshape.271), calls=%async_computation.2 | async-start | bytes 65536 | tf_op jit(solution)/shard_map/all_to_all | solution.py:143
  108.7 3.6 %copy-start = (f32[2,8,18,16,512]{4,1,3,2,0:T(8,128)}, f32[2,8,18,16,512]{4,1,3,2,0:T(8,128)S(1)}, u32[]{:S(2)}) copy-start(f32[2,8,18,16,512]{4,1,3,2,0:T(8,128)S(1)} %constant_dynamic-update-slice_fusion) | copy-start | bytes 28311556
  113.4 21.9 %collective-permute-start.3 = (f32[2,8,18,1,512]{4,1,3,2,0:T(8,128)}, f32[2,8,18,1,512]{4,1,3,2,0:T(8,128)S(1)}, u32[]{:S(2)}, u32[]{:S(2)}) collective-permute-start(f32[2,8,18,1,512]{4,1,3,2,0:T(8,128)} %get-tuple-element.85), channel_id=1, source_target_pairs={{1,0},{2,1},{3,2},{4,3},{5,4},{6,5},{7,6},{9,8},{10,9},{11,10},{12... | collective-permute-start | bytes 1769480 | tf_op jit(solution)/shard_map/ppermute | solution.py:19
  115.6 19.7 %collective-permute-start.2 = (f32[2,8,18,1,512]{4,1,3,2,0:T(8,128)}, f32[2,8,18,1,512]{4,1,3,2,0:T(8,128)S(1)}, u32[]{:S(2)}, u32[]{:S(2)}) collective-permute-start(f32[2,8,18,1,512]{4,1,3,2,0:T(8,128)} %get-tuple-element.84), channel_id=1, source_target_pairs={{0,1},{1,2},{2,3},{3,4},{4,5},{5,6},{6,7},{8,9},{9,10},{10,11},{11... | collective-permute-start | bytes 1769480 | tf_op jit(solution)/shard_map/ppermute | solution.py:18
  120.2 11.7 %all-to-all-start.1 = ((f32[32,1,256]{2,1,0:T(1,128)}), f32[32,1,256]{2,1,0:T(1,128)S(1)}, u32[]{:S(2)}, u32[]{:S(2)}) async-start(f32[32,1,256]{2,1,0:T(1,128)} %reshape.269), calls=%async_computation.1 | async-start | bytes 65536 | tf_op jit(solution)/shard_map/all_to_all | solution.py:154
where the time goes:
time: 279 us; the launch traced here: 276 us
  local copies, waits for them, and re-layouts  110 us (39%)
  other arithmetic  99.8 us (36%)
  starting transfers between devices  29.8 us (11%)
  blocking collectives  11.1 us (4%)
  loops' own time  10.8 us (4%)
  matrix products  5.76 us (2%)
  waiting for transfers between devices  4.73 us (2%)
  between operations  4.08 us (1%)
    add x1, other arithmetic, stencil_apply(): return scales[0] * stiffness - scales[1] * volume + scales[2] * turned  70.4 us
    unnamed x30, local copies, waits for them, and re-layouts  45.5 us
    scatter-add x1, local copies, waits for them, and re-layouts, on_device(): volume_out = operated.at[:, :, :, :, -1].add(cell_add)  42.6 us
    concatenate x1, other arithmetic, extended(): value = jnp.concatenate([before, value, after], axis=dim)  11.8 us
    psum x1, blocking collectives, on_device(): whole_rows = lax.psum(partial_rows, 'narrow')  11.1 us
    another operation x3, loops' own time, on_device(): lax.cond(level_index < highest, partial(level_product, level_index, block...  10.8 us
    slice x1, other arithmetic, stencil_apply(): turned = jnp.stack([volume[1], -volume[0]])  8.39 us
    ppermute x2, starting transfers between devices, extended(): before = lax.ppermute(last, axis, up)  8.14 us
  transfers between devices with their start and end apart: 7, of which 1 were waited for; matrix products, arithmetic and copies ran while one was open for 20% of the time, Pallas kernels for 0%

commit v1 on v0

v1 whole, which is shorter than its diff:
```python
import functools

import jax
import jax.numpy as jnp
from jax import lax
from jax.experimental import pallas as pl
from jax.experimental.pallas import tpu as pltpu
from jax.sharding import PartitionSpec as P

UMAX = 4
BOTH = ("wide", "narrow")


def shifts(axis):
    peers = lax.axis_size(axis)
    up = [(i, i + 1) for i in range(peers - 1)]
    return up, [(j, i) for i, j in up]


def bem_kernel(keep_ref, next_ref, density_ref, matrix_ref, out_ref, *, groups, width):
    step = pl.program_id(0)
    waves = density_ref.shape[1]
    rows = matrix_ref.shape[2]
    lane = lax.broadcasted_iota(jnp.int32, (2 * waves, width), 1)
    total = jnp.zeros((2 * waves, 2 * rows), jnp.float32)
    for g in range(groups):
        columns = pl.ds(g * width, width)
        own = density_ref[:, :, columns].reshape(2 * waves, width)
        after = jnp.where(lane == width - 1, own, pltpu.roll(own, width - 1, axis=1))
        for level in range(UMAX):
            at = step * groups + g
            fine = keep_ref[level, at] * own + next_ref[level, at] * after
            matrix = matrix_ref[:, level, :, columns].reshape(2 * rows, width)
            total = total + lax.dot_general(
                fine.astype(jnp.bfloat16),
                matrix,
                (((1,), (1,)), ((), ())),
                preferred_element_type=jnp.float32,
            )
    real = total[:waves, :rows] - total[waves:, rows:]
    imag = total[waves:, :rows] + total[:waves, rows:]
    packed = jnp.concatenate([real, imag], axis=1)

    @pl.when(step == 0)
    def _():
        out_ref[...] = packed

    @pl.when(step > 0)
    def _():
        out_ref[...] += packed


def bem_partial(density, boundary_matrix, upsample):
    parts, waves, columns = density.shape
    rows = boundary_matrix.shape[2]
    blocks = upsample.shape[0]
    width = columns // blocks
    groups = 4 if blocks % 4 == 0 else 1
    factor = upsample.astype(jnp.float32)[None, :]
    level = jnp.arange(UMAX, dtype=jnp.int32)[:, None]
    blend = level.astype(jnp.float32) / factor
    used = level < upsample[None, :]
    keep = jnp.where(used, (1.0 - blend) / factor, 0.0)
    following = jnp.where(used, blend / factor, 0.0)


    return pl.pallas_call(
        functools.partial(bem_kernel, groups=groups, width=width),
        grid=(blocks // groups,),
        in_specs=[
            pl.BlockSpec(memory_space=pltpu.SMEM),
            pl.BlockSpec(memory_space=pltpu.SMEM),
            pl.BlockSpec((parts, waves, groups * width), lambda i: (0, 0, i)),
            pl.BlockSpec((2, UMAX, rows, groups * width), lambda i: (0, 0, 0, i)),
        ],
        out_specs=pl.BlockSpec((waves, 2 * rows), lambda i: (0, 0)),
        out_shape=jax.ShapeDtypeStruct((waves, 2 * rows), jnp.float32),
        compiler_params=pltpu.CompilerParams(
            vmem_limit_bytes=40 * 1024 * 1024, dimension_semantics=("arbitrary",)
        ),
        cost_estimate=pl.CostEstimate(
            flops=2 * UMAX * 4 * waves * rows * columns,
            bytes_accessed=boundary_matrix.size * 2 + density.size * 4,
            transcendentals=0,
        ),
        name="boundary_product",
    )(keep, following, density, boundary_matrix)


def stencil_kernel(
    volume_ref, x_lo, x_hi, y_lo, y_hi, scale_ref, add_ref, out_ref, across_ref
):
    wave = pl.program_id(0)
    waves = pl.num_programs(0)
    size_x, size_y, size_z = volume_ref.shape[2:]
    shape = (size_y, size_z)
    row = lax.broadcasted_iota(jnp.int32, shape, 0)
    lane = lax.broadcasted_iota(jnp.int32, shape, 1)
    channel_lane = lax.broadcasted_iota(jnp.int32, (size_y, add_ref.shape[1]), 1)

    def sum_y(plane, part, at):
        before = y_lo[part, 0, pl.ds(at, 1), :]
        after = y_hi[part, 0, pl.ds(at, 1), :]
        up = jnp.where(row == 0, before, pltpu.roll(plane, 1, axis=0))
        down = jnp.where(row == size_y - 1, after, pltpu.roll(plane, size_y - 1, axis=0))
        return up + down

    for part in range(2):
        across_ref[part, 0] = sum_y(x_lo[part, 0], part, 0)
        across_ref[part, size_x + 1] = sum_y(x_hi[part, 0], part, size_x + 1)

    def first(x, carry):
        for part in range(2):
            across_ref[part, x + 1] = sum_y(volume_ref[part, 0, x], part, x + 1)
        return carry

    lax.fori_loop(0, size_x, first, 0)

    def emit(x, before, after):
        scale0 = scale_ref[0, x].astype(jnp.float32)
        scale1 = scale_ref[1, x].astype(jnp.float32)
        scale2 = scale_ref[2, x].astype(jnp.float32)
        own = [volume_ref[part, 0, x] for part in range(2)]
        for part in range(2):
            outer = across_ref[part, x] + across_ref[part, x + 2]
            inner = outer + 2.0 * (before[part] + after[part] + across_ref[part, x + 1])
            left = jnp.where(lane == 0, 0.0, pltpu.roll(inner, 1, axis=1))
            right = jnp.where(lane == size_z - 1, 0.0, pltpu.roll(inner, size_z - 1, axis=1))
            total = left + right + 2.0 * outer
            stiffness = (8.0 / 3.0) * own[part] - total * (1.0 / 12.0)
            turned = own[1] if part == 0 else -own[0]
            value = scale0 * stiffness - scale1 * own[part] + scale2 * turned
            tile = add_ref[pl.ds(x * size_y, size_y), :]
            added = jnp.sum(
                jnp.where(channel_lane == part * waves + wave, tile, 0.0), axis=1, keepdims=True
            )
            out_ref[part, 0, x] = value + jnp.where(lane == size_z - 1, added, 0.0)

    both = range(2)
    emit(0, [x_lo[p, 0] for p in both], [volume_ref[p, 0, 1] for p in both])

    def second(x, carry):
        emit(
            x,
            [volume_ref[p, 0, x - 1] for p in both],
            [volume_ref[p, 0, x + 1] for p in both],
        )
        return carry

    lax.fori_loop(1, size_x - 1, second, 0)
    emit(
        size_x - 1,
        [volume_ref[p, 0, size_x - 2] for p in both],
        [x_hi[p, 0] for p in both],
    )


def stencil(volume, x_lo, x_hi, y_lo, y_hi, coefficients, cell_add):
    parts, waves, size_x, size_y, size_z = volume.shape
    whole = pl.BlockSpec((parts, 1, size_x, size_y, size_z), lambda w: (0, w, 0, 0, 0))
    face_x = pl.BlockSpec((parts, 1, size_y, size_z), lambda w: (0, w, 0, 0))
    face_y = pl.BlockSpec((parts, 1, size_x + 2, size_z), lambda w: (0, w, 0, 0))
    return pl.pallas_call(
        stencil_kernel,
        grid=(waves,),
        in_specs=[
            whole,
            face_x,
            face_x,
            face_y,
            face_y,
            pl.BlockSpec(coefficients.shape, lambda w: (0, 0, 0, 0)),
            pl.BlockSpec(cell_add.shape, lambda w: (0, 0)),
        ],
        out_specs=whole,
        out_shape=jax.ShapeDtypeStruct(volume.shape, jnp.float32),
        scratch_shapes=[pltpu.VMEM((parts, size_x + 2, size_y, size_z), jnp.float32)],
        compiler_params=pltpu.CompilerParams(
            vmem_limit_bytes=40 * 1024 * 1024, dimension_semantics=("arbitrary",)
        ),
        cost_estimate=pl.CostEstimate(
            flops=volume.size * 40, bytes_accessed=volume.size * 8, transcendentals=0
        ),
        name="volume_rows",
    )(volume, x_lo, x_hi, y_lo, y_hi, coefficients, cell_add)


def on_device(
    volume_field,
    coefficients,
    density,
    boundary_matrix,
    upsample,
    trace_cell,
    trace_row,
    slot_counts,
):
    parts, waves, size_x, size_y, size_z = volume_field.shape
    n_wide, n_narrow = lax.axis_size("wide"), lax.axis_size("narrow")
    group_rows = boundary_matrix.shape[2]
    all_rows = n_wide * group_rows
    rows_each = group_rows // n_narrow

    up, down = shifts("wide")
    x_lo = lax.ppermute(volume_field[:, :, -1], "wide", up)
    x_hi = lax.ppermute(volume_field[:, :, 0], "wide", down)

    def y_face(at):
        return jnp.concatenate(
            [x_lo[:, :, at][:, :, None], volume_field[:, :, :, at], x_hi[:, :, at][:, :, None]],
            axis=2,
        )

    up, down = shifts("narrow")
    y_lo = lax.ppermute(y_face(size_y - 1), "narrow", up)
    y_hi = lax.ppermute(y_face(0), "narrow", down)

    slots = trace_row.shape[2]
    live = jnp.arange(slots, dtype=jnp.int32) < slot_counts.reshape(())
    slot_rows = jnp.where(live, trace_row.reshape(slots), -1)
    slot_cells = trace_cell.reshape(slots)
    row_hot = (slot_rows[None, :] == jnp.arange(all_rows, dtype=jnp.int32)[:, None]).astype(
        jnp.bfloat16
    )
    cell_hot = (
        slot_cells[None, :] == jnp.arange(size_x * size_y, dtype=jnp.int32)[:, None]
    ).astype(jnp.bfloat16)
    counts = lax.dot_general(
        cell_hot, row_hot, (((1,), (1,)), ((), ())), preferred_element_type=jnp.float32
    )
    top = volume_field[:, :, :, :, -1].reshape(parts * waves, size_x * size_y)
    trace_part = jnp.dot(top, counts, precision=lax.Precision.HIGHEST)
    trace_part = trace_part.reshape(parts * waves, n_wide * n_narrow, rows_each)
    trace_part = trace_part.transpose(1, 0, 2).reshape(n_wide * n_narrow, -1)
    trace_sum = lax.psum_scatter(trace_part, BOTH, scatter_dimension=0, tiled=True)
    trace_sum = trace_sum.reshape(parts * waves, rows_each)

    partial_rows = bem_partial(density, boundary_matrix, upsample)
    gathered = lax.all_gather(partial_rows, BOTH, axis=0, tiled=False)
    summed = jnp.sum(gathered.reshape(n_wide, n_narrow, waves, 2, group_rows), axis=1)
    bem_rows = summed.transpose(2, 1, 0, 3).reshape(parts * waves, all_rows)
    start = (lax.axis_index("wide") * n_narrow + lax.axis_index("narrow")) * rows_each
    own_rows = lax.dynamic_slice_in_dim(bem_rows, start, rows_each, 1)
    boundary_out = (own_rows - 0.25 * trace_sum).reshape(parts, waves, rows_each)
    cell_add = lax.dot_general(
        counts, bem_rows, (((1,), (1,)), ((), ())), precision=lax.Precision.HIGHEST
    )
    volume_out = stencil(volume_field, x_lo, x_hi, y_lo, y_hi, coefficients, cell_add)
    return (volume_out, boundary_out)


def solution(mesh):
    return jax.shard_map(
        on_device,
        mesh=mesh,
        in_specs=(
            P(None, None, "wide", "narrow", None),
            P(None, "wide", "narrow", None),
            P(None, None, "narrow"),
            P(None, None, "wide", "narrow"),
            P("narrow"),
            P("wide", "narrow", None),
            P("wide", "narrow", None),
            P("wide", "narrow"),
        ),
        out_specs=(P(None, None, "wide", "narrow", None), P(None, None, ("wide", "narrow"))),
        check_vma=False,
    )
```

time: 279 us -> 147 us (0.53)
  other arithmetic: 99.8 us -> 3.13 us
  local copies, waits for them, and re-layouts: 110 us -> 21.7 us
  blocking collectives: 11.1 us -> 80.5 us
  Pallas kernels: 0 us -> 26.1 us
  starting transfers between devices: 29.8 us -> 11.2 us
  loops' own time: 10.8 us -> 0 us
  matrix products: 5.76 us -> 0.82 us
  waiting for transfers between devices: 4.73 us -> 0.01 us
    add x2 -> x0, other arithmetic: 73.9 us -> none  [the longest x1 70.4 us: stencil_apply(): return scales[0] * stiffness - scales[1] * volume + scales[2] * turned]
    scatter-add x1 -> x0, local copies, waits for them, and re-layouts: 42.6 us -> none  [on_device(): volume_out = operated.at[:, :, :, :, -1].add(cell_add)]
    all_gather x0 -> x1, blocking collectives: none -> 41.5 us  [on_device(): gathered = lax.all_gather(partial_rows, BOTH, axis=0, tiled=False)]
    unnamed x0 -> x1, blocking collectives: none -> 39 us
    unnamed x30 -> x14, local copies, waits for them, and re-layouts: 45.5 us -> 8.43 us
    pallas_call x0 -> x2, Pallas kernels: none -> 26.1 us  [the longest x1 21.6 us: stencil(): pl.pallas_call(stencil_kernel, grid=(waves,), in_specs=[whole, face_x, fa...]
    all_to_all x3 -> x0, starting transfers between devices: 18.3 us -> none  [the longest x1 7.7 us: on_device(): lax.all_to_all(send_rows, ('wide', 'narrow'), split_axis=0, concat_axis=0...]
    concatenate x3 -> x2, other arithmetic: 12.9 us -> 0.08 us  [y_face(): jnp.concatenate([x_lo[:, :, at][:, :, None], volume_field[:, :, :, at], x...]
  transfers between devices with their start and end apart: 7 -> 4, of which waited for: 1 -> 0; matrix products, arithmetic and copies ran while one was open for 20% -> 10% of each run, Pallas kernels for 0% -> 3%
where the time goes in v1:
time: 147 us; the launch traced here: 145 us
  blocking collectives  80.5 us (55%)
  Pallas kernels  26.1 us (18%)
  local copies, waits for them, and re-layouts  21.7 us (15%)
  starting transfers between devices  11.2 us (8%)
  other arithmetic  3.13 us (2%)
  between operations  1.59 us (1%)
    all_gather x1, blocking collectives, on_device(): gathered = lax.all_gather(partial_rows, BOTH, axis=0, tiled=False)  41.5 us
    unnamed x1, blocking collectives  39 us
    pallas_call x1, Pallas kernels, stencil(): pl.pallas_call(stencil_kernel, grid=(waves,), in_specs=[whole, face_x, fa...  21.6 us
    unnamed x14, local copies, waits for them, and re-layouts  8.43 us
    slice x1, local copies, waits for them, and re-layouts, y_face(): volume_field[:, :, :, at]  4.61 us
    ppermute x1, starting transfers between devices, on_device(): x_lo = lax.ppermute(volume_field[:, :, -1], 'wide', up)  4.6 us
    pallas_call x1, Pallas kernels, bem_partial(): pl.pallas_call(functools.partial(bem_kernel, groups=groups, width=width),...  4.43 us
    ppermute x1, starting transfers between devices, on_device(): y_hi = lax.ppermute(y_face(0), 'narrow', down)  3.22 us
  transfers between devices with their start and end apart: 4, of which 0 were waited for; matrix products, arithmetic and copies ran while one was open for 10% of the time, Pallas kernels for 3%

profile of v1, /device:TPU:1, one launch (start us, length us, event | category | flops | bytes accessed | tf_op | source)
XLA Modules:
  0.0 145.0 jit_solution(2404736730161781799)
XLA Ops:
  0.6 2.3 %slice_bitcast_fusion = (f32[2,8,16,512]{3,2,1,0:T(8,128)}, f32[2,8,16,512]{3,2,1,0:T(8,128)}) fusion(f32[2,8,16,16,512]{4,3,2,1,0:T(8,128)} %volume_ref.1), kind=kLoop, calls=%fused_computation.6 | loop fusion | bytes 2097152 | tf_op jit(solution)/shard_map/squeeze | solution.py:206
  2.9 1.4 collective-permute-start.1
  4.3 4.6 %collective-permute-start = (f32[2,8,16,512]{3,2,1,0:T(8,128)}, f32[2,8,16,512]{3,2,1,0:T(8,128)S(1)}, u32[]{:S(2)}, u32[]{:S(2)}) collective-permute-start(f32[2,8,16,512]{3,2,1,0:T(8,128)} %get-tuple-element.13), channel_id=1, source_target_pairs={{0,8},{8,16},{16,24},{1,9},{9,17},{17,25},{2,10},{10,18},{18,26},{... | collective-permute-start | bytes 1572872 | tf_op jit(solution)/shard_map/ppermute | solution.py:205
  9.0 0.7 convert_element_type.16
  9.6 0.7 convert_multiply_fusion
  10.3 2.8 %slice_reduce_fusion = f32[2,8,16,16]{3,2,1,0:T(8,128)S(1)} fusion(f32[2,8,16,16,512]{4,3,2,1,0:T(8,128)} %volume_ref.1), kind=kLoop, calls=%fused_computation | loop fusion | bytes 32768 | tf_op jit(solution)/shard_map/slice | solution.py:231
  13.1 4.6 %fusion.6 = (f32[2,8,16,1,512]{4,3,2,1,0:T(1,128)S(1)}, f32[2,8,16,1,512]{4,3,2,1,0:T(1,128)S(1)}) fusion(f32[2,8,16,16,512]{4,3,2,1,0:T(8,128)} %volume_ref.1), kind=kLoop, calls=%fused_computation.24 | loop fusion | bytes 2097152 | tf_op jit(solution)/shard_map/slice | solution.py:210
  17.7 0.7 divide_select_fusion
  18.4 3.4 %copy-done.1 = bf16[2,4,64,8192]{3,2,1,0:T(8,128)(2,1)S(1)} copy-done((bf16[2,4,64,8192]{3,2,1,0:T(8,128)(2,1)S(1)}, bf16[2,4,64,8192]{3,2,1,0:T(8,128)(2,1)}, u32[]{:S(2)}) %copy-start.1) | copy-done | bytes 8388632
  21.8 1.0 copy-done.3
  22.8 4.4 %boundary_product.1 = f32[8,128]{1,0:T(8,128)S(1)} custom-call(f32[4,16]{1,0:T(4,128)S(1)} %get-tuple-element.19.keep_ref, f32[4,16]{1,0:T(4,128)S(1)} %get-tuple-element.18.next_ref, f32[2,8,8192]{2,1,0:T(8,128)S(1)} %copy-done.3, bf16[2,4,64,8192]{3,2,1,0:T(8,128)(2,1)S(1)} %copy-done.1), custom_call_target="tpu_custom_call" | custom-call | flops 134217728 | bytes 8912896 | tf_op jit(solution)/shard_map/boundary_product/pallas_call | solution.py:67
  28.0 41.5 %all-gather = f32[256,128]{1,0:T(8,128)S(1)} all-gather(f32[8,128]{1,0:T(8,128)S(1)} %boundary_product.1), channel_id=2, replica_groups=mesh['wide'=4,'narrow'=8] {'wide','narrow'}, dimensions={0}, use_global_device_ids=true | all-gather | bytes 135168 | tf_op jit(solution)/shard_map/all_gather | solution.py:239
  70.0 0.3 copy.68
  70.3 0.3 copy.69
  71.1 1.9 %collective-permute-start.2 = (f32[2,8,18,512]{3,1,2,0:T(8,128)S(1)}, f32[2,8,18,512]{3,1,2,0:T(8,128)}, u32[]{:S(2)}, u32[]{:S(2)}) collective-permute-start(f32[2,8,18,512]{3,1,2,0:T(8,128)S(1)} %pad_maximum_fusion), channel_id=1, source_target_pairs={{0,1},{1,2},{2,3},{3,4},{4,5},{5,6},{6,7},{8,9},{9,10},{10,11},{11... | collective-permute-start | bytes 1769480 | tf_op jit(solution)/shard_map/ppermute | solution.py:215
  73.1 3.2 %collective-permute-start.3 = (f32[2,8,18,512]{3,1,2,0:T(8,128)S(1)}, f32[2,8,18,512]{3,1,2,0:T(8,128)}, u32[]{:S(2)}, u32[]{:S(2)}) collective-permute-start(f32[2,8,18,512]{3,1,2,0:T(8,128)S(1)} %pad_maximum_fusion.1), channel_id=1, source_target_pairs={{1,0},{2,1},{3,2},{4,3},{5,4},{6,5},{7,6},{9,8},{10,9},{11,10},{12... | collective-permute-start | bytes 1769480 | tf_op jit(solution)/shard_map/ppermute | solution.py:216
  76.3 0.2 convolution_bitcast_fusion
  76.8 39.0 %all-reduce = f32[32,128]{0,1:T(8,128)S(1)} all-reduce(f32[32,128]{0,1:T(8,128)S(1)} %bitcast.38), channel_id=3, replica_groups=mesh['wide'=4,'narrow'=8] {'wide','narrow'}, use_global_device_ids=true, to_apply=%region_1.2.clone | all-reduce | flops 4096 | bytes 32768
  116.0 0.7 subtract_bitcast_fusion
  116.8 0.3 fusion.9.add_ref
  117.1 1.4 copy.51.y_lo
  118.5 1.4 copy.52.y_hi
  120.0 3.4 %copy-done = f32[2,8,16,16,512]{4,3,2,1,0:T(8,128)S(1)} copy-done((f32[2,8,16,16,512]{4,3,2,1,0:T(8,128)S(1)}, f32[2,8,16,16,512]{4,3,2,1,0:T(8,128)}, u32[]{:S(2)}) %copy-start) | copy-done | bytes 8388632
  123.4 21.6 %volume_rows.1 = f32[2,8,16,16,512]{4,3,2,1,0:T(8,128)} custom-call(f32[2,8,16,16,512]{4,3,2,1,0:T(8,128)S(1)} %copy-done, f32[2,8,16,512]{3,2,1,0:T(8,128)S(1)} %collective-permute-done.x_lo, f32[2,8,16,512]{3,2,1,0:T(8,128)S(1)} %collective-permute-done.1.x_hi, f32[2,8,18,512]{3,2,1,0:T(8,128)S(1)} %copy.51.y_lo, f32[2,8,18,512]{3,2,1,0:T(8,128)S(1)} %copy.52.y_hi, ...), custom_call_target="tpu_custom_call" | custom-call | flops 83886080 | bytes 16777216 | tf_op jit(solution)/shard_map/volume_rows/pallas_call | solution.py:163
  (33 shorter events, 1.5 us)
Async XLA Ops:
  0.6 27.3 %copy-start.5 = (s32[1,1,256]{2,1,0:T(1,128)S(1)}, s32[1,1,256]{2,1,0:T(1,128)}, u32[]{:S(2)}) copy-start(s32[1,1,256]{2,1,0:T(1,128)} %param.14) | copy-start | bytes 3076
  2.9 67.7 %copy-start.4 = (s32[1,1,256]{2,1,0:T(1,128)S(1)}, s32[1,1,256]{2,1,0:T(1,128)}, u32[]{:S(2)}) copy-start(s32[1,1,256]{2,1,0:T(1,128)} %param.13) | copy-start | bytes 3076
  2.9 68.0 %collective-permute-start.1 = (f32[2,8,16,512]{3,2,1,0:T(8,128)}, f32[2,8,16,512]{3,2,1,0:T(8,128)S(1)}, u32[]{:S(2)}, u32[]{:S(2)}) collective-permute-start(f32[2,8,16,512]{3,2,1,0:T(8,128)} %get-tuple-element.12), channel_id=1, source_target_pairs={{8,0},{16,8},{24,16},{9,1},{17,9},{25,17},{10,2},{18,10},{26,18},{... | collective-permute-start | bytes 1572872 | tf_op jit(solution)/shard_map/ppermute | solution.py:206
  4.3 66.6 %collective-permute-start = (f32[2,8,16,512]{3,2,1,0:T(8,128)}, f32[2,8,16,512]{3,2,1,0:T(8,128)S(1)}, u32[]{:S(2)}, u32[]{:S(2)}) collective-permute-start(f32[2,8,16,512]{3,2,1,0:T(8,128)} %get-tuple-element.13), channel_id=1, source_target_pairs={{0,8},{8,16},{16,24},{1,9},{9,17},{17,25},{2,10},{10,18},{18,26},{... | collective-permute-start | bytes 1572872 | tf_op jit(solution)/shard_map/ppermute | solution.py:205
  18.4 3.4 %copy-start.1 = (bf16[2,4,64,8192]{3,2,1,0:T(8,128)(2,1)S(1)}, bf16[2,4,64,8192]{3,2,1,0:T(8,128)(2,1)}, u32[]{:S(2)}) copy-start(bf16[2,4,64,8192]{3,2,1,0:T(8,128)(2,1)} %matrix_ref.1) | copy-start | bytes 25165828
  21.8 1.0 copy-start.3
  22.8 97.1 %copy-start.2 = (bf16[3,16,16,512]{3,2,1,0:T(8,128)(2,1)S(1)}, bf16[3,16,16,512]{3,2,1,0:T(8,128)(2,1)}, u32[]{:S(2)}) copy-start(bf16[3,16,16,512]{3,2,1,0:T(8,128)(2,1)} %scale_ref.1) | copy-start | bytes 2359300
  71.1 46.0 %collective-permute-start.2 = (f32[2,8,18,512]{3,1,2,0:T(8,128)S(1)}, f32[2,8,18,512]{3,1,2,0:T(8,128)}, u32[]{:S(2)}, u32[]{:S(2)}) collective-permute-start(f32[2,8,18,512]{3,1,2,0:T(8,128)S(1)} %pad_maximum_fusion), channel_id=1, source_target_pairs={{0,1},{1,2},{2,3},{3,4},{4,5},{5,6},{6,7},{8,9},{9,10},{10,11},{11... | collective-permute-start | bytes 1769480 | tf_op jit(solution)/shard_map/ppermute | solution.py:215
  73.1 45.4 %collective-permute-start.3 = (f32[2,8,18,512]{3,1,2,0:T(8,128)S(1)}, f32[2,8,18,512]{3,1,2,0:T(8,128)}, u32[]{:S(2)}, u32[]{:S(2)}) collective-permute-start(f32[2,8,18,512]{3,1,2,0:T(8,128)S(1)} %pad_maximum_fusion.1), channel_id=1, source_target_pairs={{1,0},{2,1},{3,2},{4,3},{5,4},{6,5},{7,6},{9,8},{10,9},{11,10},{12... | collective-permute-start | bytes 1769480 | tf_op jit(solution)/shard_map/ppermute | solution.py:216
  120.0 3.4 %copy-start = (f32[2,8,16,16,512]{4,3,2,1,0:T(8,128)S(1)}, f32[2,8,16,16,512]{4,3,2,1,0:T(8,128)}, u32[]{:S(2)}) copy-start(f32[2,8,16,16,512]{4,3,2,1,0:T(8,128)} %volume_ref.1) | copy-start | bytes 25165828

commit v2 on v1

--- a/solution.py
+++ b/solution.py
@@ -88,30 +88,31 @@
 
 
 def stencil_kernel(
-    volume_ref, x_lo, x_hi, y_lo, y_hi, scale_ref, add_ref, out_ref, across_ref
+    volume_ref, x_lo, x_hi, y_lo, y_hi, edge_lo, edge_hi, scale_ref, out_ref, across_ref
 ):
-    wave = pl.program_id(0)
-    waves = pl.num_programs(0)
     size_x, size_y, size_z = volume_ref.shape[2:]
     shape = (size_y, size_z)
     row = lax.broadcasted_iota(jnp.int32, shape, 0)
     lane = lax.broadcasted_iota(jnp.int32, shape, 1)
-    channel_lane = lax.broadcasted_iota(jnp.int32, (size_y, add_ref.shape[1]), 1)
-
-    def sum_y(plane, part, at):
-        before = y_lo[part, 0, pl.ds(at, 1), :]
-        after = y_hi[part, 0, pl.ds(at, 1), :]
+
+    def sum_y(plane, before, after):
         up = jnp.where(row == 0, before, pltpu.roll(plane, 1, axis=0))
         down = jnp.where(row == size_y - 1, after, pltpu.roll(plane, size_y - 1, axis=0))
         return up + down
 
     for part in range(2):
-        across_ref[part, 0] = sum_y(x_lo[part, 0], part, 0)
-        across_ref[part, size_x + 1] = sum_y(x_hi[part, 0], part, size_x + 1)
+        for side, face, at in ((0, x_lo, 0), (1, x_hi, size_x + 1)):
+            across_ref[part, at] = sum_y(
+                face[part, 0], edge_lo[part, 0, side : side + 1], edge_hi[part, 0, side : side + 1]
+            )
 
     def first(x, carry):
         for part in range(2):
-            across_ref[part, x + 1] = sum_y(volume_ref[part, 0, x], part, x + 1)
+            across_ref[part, x + 1] = sum_y(
+                volume_ref[part, 0, x],
+                y_lo[part, 0, pl.ds(x, 1), :],
+                y_hi[part, 0, pl.ds(x, 1), :],
+            )
         return carry
 
     lax.fori_loop(0, size_x, first, 0)
@@ -129,12 +130,7 @@
             total = left + right + 2.0 * outer
             stiffness = (8.0 / 3.0) * own[part] - total * (1.0 / 12.0)
             turned = own[1] if part == 0 else -own[0]
-            value = scale0 * stiffness - scale1 * own[part] + scale2 * turned
-            tile = add_ref[pl.ds(x * size_y, size_y), :]
-            added = jnp.sum(
-                jnp.where(channel_lane == part * waves + wave, tile, 0.0), axis=1, keepdims=True
-            )
-            out_ref[part, 0, x] = value + jnp.where(lane == size_z - 1, added, 0.0)
+            out_ref[part, 0, x] = scale0 * stiffness - scale1 * own[part] + scale2 * turned
 
     both = range(2)
     emit(0, [x_lo[p, 0] for p in both], [volume_ref[p, 0, 1] for p in both])
@@ -155,11 +151,48 @@
     )
 
 
-def stencil(volume, x_lo, x_hi, y_lo, y_hi, coefficients, cell_add):
+def top_kernel(operated_ref, add_ref, out_ref):
+    wave = pl.program_id(0)
+    waves = pl.num_programs(0)
+    size_x, size_y, size_z = operated_ref.shape[2:]
+    cells = size_x * size_y
+    channel = lax.broadcasted_iota(jnp.int32, (cells, add_ref.shape[1]), 1)
+    lane = lax.broadcasted_iota(jnp.int32, (cells, size_z), 1)
+    for part in range(2):
+        added = jnp.sum(
+            jnp.where(channel == part * waves + wave, add_ref[...], 0.0), axis=1, keepdims=True
+        )
+        own = operated_ref[part, 0].reshape(cells, size_z)
+        total = own + jnp.where(lane == size_z - 1, added, 0.0)
+        out_ref[part, 0] = total.reshape(size_x, size_y, size_z)
+
+
+def add_top(operated, cell_add):
+    parts, waves, size_x, size_y, size_z = operated.shape
+    depth = 128
+    block = pl.BlockSpec(
+        (parts, 1, size_x, size_y, depth), lambda w: (0, w, 0, 0, size_z // depth - 1)
+    )
+    return pl.pallas_call(
+        top_kernel,
+        grid=(waves,),
+        in_specs=[block, pl.BlockSpec(cell_add.shape, lambda w: (0, 0))],
+        out_specs=block,
+        out_shape=jax.ShapeDtypeStruct(operated.shape, jnp.float32),
+        input_output_aliases={0: 0},
+        cost_estimate=pl.CostEstimate(
+            flops=operated.size, bytes_accessed=operated.size * 2, transcendentals=0
+        ),
+        name="slot_rows",
+    )(operated, cell_add)
+
+
+def stencil(volume, x_lo, x_hi, y_lo, y_hi, edge_lo, edge_hi, coefficients):
     parts, waves, size_x, size_y, size_z = volume.shape
     whole = pl.BlockSpec((parts, 1, size_x, size_y, size_z), lambda w: (0, w, 0, 0, 0))
     face_x = pl.BlockSpec((parts, 1, size_y, size_z), lambda w: (0, w, 0, 0))
-    face_y = pl.BlockSpec((parts, 1, size_x + 2, size_z), lambda w: (0, w, 0, 0))
+    face_y = pl.BlockSpec((parts, 1, size_x, size_z), lambda w: (0, w, 0, 0))
+    edge = pl.BlockSpec((parts, 1, 2, size_z), lambda w: (0, w, 0, 0))
     return pl.pallas_call(
         stencil_kernel,
         grid=(waves,),
@@ -169,8 +202,9 @@
             face_x,
             face_y,
             face_y,
+            edge,
+            edge,
             pl.BlockSpec(coefficients.shape, lambda w: (0, 0, 0, 0)),
-            pl.BlockSpec(cell_add.shape, lambda w: (0, 0)),
         ],
         out_specs=whole,
         out_shape=jax.ShapeDtypeStruct(volume.shape, jnp.float32),
@@ -182,7 +216,7 @@
             flops=volume.size * 40, bytes_accessed=volume.size * 8, transcendentals=0
         ),
         name="volume_rows",
-    )(volume, x_lo, x_hi, y_lo, y_hi, coefficients, cell_add)
+    )(volume, x_lo, x_hi, y_lo, y_hi, edge_lo, edge_hi, coefficients)
 
 
 def on_device(
@@ -205,15 +239,18 @@
     x_lo = lax.ppermute(volume_field[:, :, -1], "wide", up)
     x_hi = lax.ppermute(volume_field[:, :, 0], "wide", down)
 
-    def y_face(at):
-        return jnp.concatenate(
-            [x_lo[:, :, at][:, :, None], volume_field[:, :, :, at], x_hi[:, :, at][:, :, None]],
-            axis=2,
-        )
-
-    up, down = shifts("narrow")
-    y_lo = lax.ppermute(y_face(size_y - 1), "narrow", up)
-    y_hi = lax.ppermute(y_face(0), "narrow", down)
+    up_y, down_y = shifts("narrow")
+    y_lo = lax.ppermute(volume_field[:, :, :, -1], "narrow", up_y)
+    y_hi = lax.ppermute(volume_field[:, :, :, 0], "narrow", down_y)
+
+    partial_rows = bem_partial(density, boundary_matrix, upsample)
+    x_lo, x_hi, partial_rows = lax.optimization_barrier((x_lo, x_hi, partial_rows))
+
+    def edges(at):
+        return jnp.stack([x_lo[:, :, at], x_hi[:, :, at]], axis=2)
+
+    edge_lo = lax.ppermute(edges(size_y - 1), "narrow", up_y)
+    edge_hi = lax.ppermute(edges(0), "narrow", down_y)
 
     slots = trace_row.shape[2]
     live = jnp.arange(slots, dtype=jnp.int32) < slot_counts.reshape(())
@@ -232,11 +269,16 @@
     trace_part = jnp.dot(top, counts, precision=lax.Precision.HIGHEST)
     trace_part = trace_part.reshape(parts * waves, n_wide * n_narrow, rows_each)
     trace_part = trace_part.transpose(1, 0, 2).reshape(n_wide * n_narrow, -1)
-    trace_sum = lax.psum_scatter(trace_part, BOTH, scatter_dimension=0, tiled=True)
-    trace_sum = trace_sum.reshape(parts * waves, rows_each)
-
-    partial_rows = bem_partial(density, boundary_matrix, upsample)
-    gathered = lax.all_gather(partial_rows, BOTH, axis=0, tiled=False)
+    devices = n_wide * n_narrow
+    flat = partial_rows.size
+    outgoing = jnp.concatenate(
+        [jnp.broadcast_to(partial_rows.reshape(1, flat), (devices, flat)), trace_part], axis=1
+    )
+    arrived = lax.all_to_all(
+        outgoing.reshape(devices, 1, -1), BOTH, split_axis=0, concat_axis=0, tiled=True
+    ).reshape(devices, -1)
+    trace_sum = jnp.sum(arrived[:, flat:], axis=0).reshape(parts * waves, rows_each)
+    gathered = arrived[:, :flat]
     summed = jnp.sum(gathered.reshape(n_wide, n_narrow, waves, 2, group_rows), axis=1)
     bem_rows = summed.transpose(2, 1, 0, 3).reshape(parts * waves, all_rows)
     start = (lax.axis_index("wide") * n_narrow + lax.axis_index("narrow")) * rows_each
@@ -245,7 +287,8 @@
     cell_add = lax.dot_general(
         counts, bem_rows, (((1,), (1,)), ((), ())), precision=lax.Precision.HIGHEST
     )
-    volume_out = stencil(volume_field, x_lo, x_hi, y_lo, y_hi, coefficients, cell_add)
+    operated = stencil(volume_field, x_lo, x_hi, y_lo, y_hi, edge_lo, edge_hi, coefficients)
+    volume_out = add_top(operated, cell_add)
     return (volume_out, boundary_out)
 
 

time: 147 us -> 90.7 us (0.62)
  blocking collectives: 80.5 us -> 0 us
  starting transfers between devices: 11.2 us -> 26.5 us
  Pallas kernels: 26.1 us -> 30.6 us
  waiting for transfers between devices: 0.01 us -> 3.66 us
    all_gather x1 -> x0, blocking collectives: 41.5 us -> none  [on_device(): gathered = lax.all_gather(partial_rows, BOTH, axis=0, tiled=False)]
    unnamed x1 -> x0, blocking collectives: 39 us -> none
    all_to_all x0 -> x1, starting transfers between devices: none -> 9.25 us  [on_device(): lax.all_to_all(outgoing.reshape(devices, 1, -1), BOTH, split_axis=0, conc...]
    ppermute x2 -> x4, starting transfers between devices: 5.14 us -> 12 us  [the longest x1 4.58 us: on_device(): y_lo = lax.ppermute(volume_field[:, :, :, -1], 'narrow', up_y)]
    pallas_call x0 -> x1, Pallas kernels: none -> 6.14 us  [add_top(): pl.pallas_call(top_kernel, grid=(waves,), in_specs=[block, pl.BlockSpec(c...]
    ppermute x2 -> x4, waiting for transfers between devices: 0.01 us -> 3.63 us  [the longest x1 3.62 us: on_device(): edge_hi = lax.ppermute(edges(0), 'narrow', down_y)]
    ppermute x2 -> x0, local copies, waits for them, and re-layouts: 2.84 us -> none  [the longest x1 1.42 us: on_device(): y_lo = lax.ppermute(y_face(size_y - 1), 'narrow', up)]
    reshape x0 -> x2, local copies, waits for them, and re-layouts: none -> 1.65 us  [the longest x1 0.89 us: on_device(): trace_part = trace_part.transpose(1, 0, 2).reshape(n_wide * n_narrow, -1)]
  transfers between devices with their start and end apart: 4 -> 7, of which waited for: 0 -> 1; matrix products, arithmetic and copies ran while one was open for 10% -> 14% of each run, Pallas kernels for 3% -> 27%
where the time goes in v2:
time: 90.7 us; the launch traced here: 90 us
  Pallas kernels  30.6 us (34%)
  starting transfers between devices  26.5 us (29%)
  local copies, waits for them, and re-layouts  22 us (24%)
  waiting for transfers between devices  3.66 us (4%)
  other arithmetic  3.56 us (4%)
  matrix products  2.15 us (2%)
  between operations  1.53 us (2%)
    pallas_call x1, Pallas kernels, stencil(): pl.pallas_call(stencil_kernel, grid=(waves,), in_specs=[whole, face_x, fa...  20 us
    all_to_all x1, starting transfers between devices, on_device(): lax.all_to_all(outgoing.reshape(devices, 1, -1), BOTH, split_axis=0, conc...  9.25 us
    unnamed x17, local copies, waits for them, and re-layouts  9.17 us
    pallas_call x1, Pallas kernels, add_top(): pl.pallas_call(top_kernel, grid=(waves,), in_specs=[block, pl.BlockSpec(c...  6.14 us
    slice x1, local copies, waits for them, and re-layouts, on_device(): y_hi = lax.ppermute(volume_field[:, :, :, 0], 'narrow', down_y)  4.65 us
    ppermute x1, starting transfers between devices, on_device(): y_lo = lax.ppermute(volume_field[:, :, :, -1], 'narrow', up_y)  4.58 us
    pallas_call x1, Pallas kernels, bem_partial(): pl.pallas_call(functools.partial(bem_kernel, groups=groups, width=width),...  4.43 us
    ppermute x1, starting transfers between devices, on_device(): x_lo = lax.ppermute(volume_field[:, :, -1], 'wide', up)  4.02 us
  transfers between devices with their start and end apart: 7, of which 1 were waited for; matrix products, arithmetic and copies ran while one was open for 14% of the time, Pallas kernels for 27%

profile of v2, /device:TPU:1, one launch (start us, length us, event | category | flops | bytes accessed | tf_op | source)
XLA Modules:
  0.0 90.0 jit_solution(10357189768102648143)
XLA Ops:
  0.7 4.6 %fusion.5 = (f32[2,8,16,1,512]{4,3,2,1,0:T(1,128)S(1)}, f32[2,8,16,1,512]{4,3,2,1,0:T(1,128)S(1)}) fusion(f32[2,8,16,16,512]{4,3,2,1,0:T(8,128)} %volume_ref.1), kind=kLoop, calls=%fused_computation.26 | loop fusion | bytes 2097152 | tf_op jit(solution)/shard_map/slice | solution.py:244
  5.3 0.8 copy.70
  6.1 4.6 %collective-permute-start.2 = (f32[2,8,16,512]{3,2,1,0:T(8,128)}, f32[2,8,16,512]{3,2,1,0:T(8,128)S(1)}, u32[]{:S(2)}, u32[]{:S(2)}) collective-permute-start(f32[2,8,16,512]{3,2,1,0:T(8,128)} %bitcast.34), channel_id=1, source_target_pairs={{0,1},{1,2},{2,3},{3,4},{4,5},{5,6},{6,7},{8,9},{9,10},{10,11},{11... | collective-permute-start | bytes 1572872 | tf_op jit(solution)/shard_map/ppermute | solution.py:243
  10.8 0.8 copy.69
  11.6 1.9 %collective-permute-start.3 = (f32[2,8,16,512]{3,2,1,0:T(8,128)}, f32[2,8,16,512]{3,2,1,0:T(8,128)S(1)}, u32[]{:S(2)}, u32[]{:S(2)}) collective-permute-start(f32[2,8,16,512]{3,2,1,0:T(8,128)} %bitcast.33), channel_id=1, source_target_pairs={{1,0},{2,1},{3,2},{4,3},{5,4},{6,5},{7,6},{9,8},{10,9},{11,10},{12... | collective-permute-start | bytes 1572872 | tf_op jit(solution)/shard_map/ppermute | solution.py:244
  13.5 2.3 %slice_bitcast_fusion = (f32[2,8,16,512]{3,2,1,0:T(8,128)}, f32[2,8,16,512]{3,2,1,0:T(8,128)}) fusion(f32[2,8,16,16,512]{4,3,2,1,0:T(8,128)} %volume_ref.1), kind=kLoop, calls=%fused_computation.4 | loop fusion | bytes 2097152 | tf_op jit(solution)/shard_map/squeeze | solution.py:240
  15.8 1.3 %collective-permute-start.1 = (f32[2,8,16,512]{3,2,1,0:T(8,128)}, f32[2,8,16,512]{3,2,1,0:T(8,128)S(1)}, u32[]{:S(2)}, u32[]{:S(2)}) collective-permute-start(f32[2,8,16,512]{3,2,1,0:T(8,128)} %get-tuple-element.20), channel_id=1, source_target_pairs={{8,0},{16,8},{24,16},{9,1},{17,9},{25,17},{10,2},{18,10},{26,18},{... | collective-permute-start | bytes 1572872 | tf_op jit(solution)/shard_map/ppermute | solution.py:240
  17.1 4.0 %collective-permute-start = (f32[2,8,16,512]{3,2,1,0:T(8,128)}, f32[2,8,16,512]{3,2,1,0:T(8,128)S(1)}, u32[]{:S(2)}, u32[]{:S(2)}) collective-permute-start(f32[2,8,16,512]{3,2,1,0:T(8,128)} %get-tuple-element.21), channel_id=1, source_target_pairs={{0,8},{8,16},{16,24},{1,9},{9,17},{17,25},{2,10},{10,18},{18,26},{... | collective-permute-start | bytes 1572872 | tf_op jit(solution)/shard_map/ppermute | solution.py:239
  21.1 2.8 %slice_reduce_fusion = f32[2,8,16,16]{3,2,1,0:T(8,128)S(1)} fusion(f32[2,8,16,16,512]{4,3,2,1,0:T(8,128)} %volume_ref.1), kind=kLoop, calls=%fused_computation | loop fusion | bytes 32768 | tf_op jit(solution)/shard_map/slice | solution.py:268
  25.9 0.9 %fusion = f32[256,256]{1,0:T(8,128)S(1)} fusion(s32[256]{0:T(256)S(1)} %compare_select_fusion, s32[256]{0:T(256)} %bitcast.43), kind=kOutput, calls=%fused_computation.8 | convolution fusion | flops 33685504 | bytes 264192 | tf_op jit(solution)/shard_map/dot_general | solution.py:265
  27.8 0.7 copy.53
  28.6 0.9 copy.54
  30.2 0.7 divide_select_fusion
  30.9 3.4 %copy-done.1 = bf16[2,4,64,8192]{3,2,1,0:T(8,128)(2,1)S(1)} copy-done((bf16[2,4,64,8192]{3,2,1,0:T(8,128)(2,1)S(1)}, bf16[2,4,64,8192]{3,2,1,0:T(8,128)(2,1)}, u32[]{:S(2)}) %copy-start.1) | copy-done | bytes 8388632
  34.3 4.4 %boundary_product.1 = f32[8,128]{1,0:T(8,128)S(1)} custom-call(f32[4,16]{1,0:T(4,128)S(1)} %get-tuple-element.27.keep_ref, f32[4,16]{1,0:T(4,128)S(1)} %get-tuple-element.26.next_ref, f32[2,8,8192]{2,1,0:T(8,128)S(1)} %copy-done.3, bf16[2,4,64,8192]{3,2,1,0:T(8,128)(2,1)S(1)} %copy-done.1), custom_call_target="tpu_custom_call" | custom-call | flops 134217728 | bytes 8912896 | tf_op jit(solution)/shard_map/boundary_product/pallas_call | solution.py:67
  38.8 0.8 reshape.57
  39.5 9.2 %all-to-all-start = ((f32[32,1,1152]{2,1,0:T(1,128)}), f32[32,1,1152]{2,1,0:T(1,128)S(1)}, u32[]{:S(2)}, u32[]{:S(2)}) async-start(f32[32,1,1152]{2,1,0:T(1,128)} %reshape.57), calls=%async_computation | async-start | bytes 294912 | tf_op jit(solution)/shard_map/all_to_all | solution.py:277
  49.0 3.5 %collective-permute-start.4 = (f32[2,8,2,512]{3,2,1,0:T(2,128)S(1)}, f32[2,8,2,512]{3,2,1,0:T(2,128)S(1)}, u32[]{:S(2)}, u32[]{:S(2)}) collective-permute-start(f32[2,8,2,512]{3,2,1,0:T(2,128)S(1)} %pad_maximum_fusion.1), channel_id=1, source_target_pairs={{0,1},{1,2},{2,3},{3,4},{4,5},{5,6},{6,7},{8,9},{9,10},{10,11},{11... | collective-permute-start | bytes 196616 | tf_op jit(solution)/shard_map/ppermute | solution.py:252
  52.6 1.9 %collective-permute-start.5 = (f32[2,8,2,512]{3,2,1,0:T(2,128)S(1)}, f32[2,8,2,512]{3,2,1,0:T(2,128)S(1)}, u32[]{:S(2)}, u32[]{:S(2)}) collective-permute-start(f32[2,8,2,512]{3,2,1,0:T(2,128)S(1)} %pad_maximum_fusion.2), channel_id=1, source_target_pairs={{1,0},{2,1},{3,2},{4,3},{5,4},{6,5},{7,6},{9,8},{10,9},{11,10},{12... | collective-permute-start | bytes 196616 | tf_op jit(solution)/shard_map/ppermute | solution.py:253
  54.6 3.6 %collective-permute-done.5.edge_hi = f32[2,8,2,512]{3,2,1,0:T(2,128)S(1)} collective-permute-done((f32[2,8,2,512]{3,2,1,0:T(2,128)S(1)}, f32[2,8,2,512]{3,2,1,0:T(2,128)S(1)}, u32[]{:S(2)}, u32[]{:S(2)}) %collective-permute-start.5) | collective-permute-done | bytes 65568 | tf_op jit(solution)/shard_map/ppermute | solution.py:253
  58.2 3.4 %copy-done = f32[2,8,16,16,512]{4,3,2,1,0:T(8,128)S(1)} copy-done((f32[2,8,16,16,512]{4,3,2,1,0:T(8,128)S(1)}, f32[2,8,16,16,512]{4,3,2,1,0:T(8,128)}, u32[]{:S(2)}) %copy-start) | copy-done | bytes 8388632
  61.6 20.0 %volume_rows.1.operated_ref = f32[2,8,16,16,512]{4,3,2,1,0:T(8,128)} custom-call(f32[2,8,16,16,512]{4,3,2,1,0:T(8,128)S(1)} %copy-done, f32[2,8,16,512]{3,2,1,0:T(8,128)S(1)} %collective-permute-done.x_lo, f32[2,8,16,512]{3,2,1,0:T(8,128)S(1)} %collective-permute-done.1.x_hi, f32[2,8,16,512]{3,2,1,0:T(8,128)S(1)} %collective-permute-done.2.y_lo, ...), custom_call_target="tpu_custom_call" | custom-call | flops 83886080 | bytes 16777216 | tf_op jit(solution)/shard_map/volume_rows/pallas_call | solution.py:196
  82.2 1.0 %fusion.8.add_ref = f32[256,16]{1,0:T(8,128)} fusion(f32[256,256]{1,0:T(8,128)S(1)} %copy-done.5, f32[16,256]{1,0:T(8,128)S(1)} %reshape.60), kind=kOutput, calls=%fused_computation.29 | convolution fusion | flops 12582912 | bytes 294912 | tf_op jit(solution)/shard_map/dot_general | solution.py:287
  83.9 6.1 %slot_rows.1 = f32[2,8,16,16,512]{4,3,2,1,0:T(8,128)} custom-call(f32[2,8,16,16,512]{4,3,2,1,0:T(8,128)} %volume_rows.1.operated_ref, f32[256,16]{1,0:T(8,128)} %fusion.8.add_ref), custom_call_target="tpu_custom_call", output_to_operand_aliasing={{}: (0, {})} | custom-call | flops 2097152 | bytes 4194304 | tf_op jit(solution)/shard_map/slot_rows/pallas_call | solution.py:176
  (40 shorter events, 4.6 us)
Async XLA Ops:
  0.6 23.9 %copy-start.6 = (s32[16]{0:T(128)S(1)}, s32[16]{0:T(128)}, u32[]{:S(2)}) copy-start(s32[16]{0:T(128)} %param.12) | copy-start | bytes 196
  0.6 30.3 %copy-start.3 = (f32[2,8,8192]{2,1,0:T(8,128)S(1)}, f32[2,8,8192]{2,1,0:T(8,128)}, u32[]{:S(2)}) copy-start(f32[2,8,8192]{2,1,0:T(8,128)} %density_ref.1) | copy-start | bytes 1572868
  6.1 48.4 %collective-permute-start.2 = (f32[2,8,16,512]{3,2,1,0:T(8,128)}, f32[2,8,16,512]{3,2,1,0:T(8,128)S(1)}, u32[]{:S(2)}, u32[]{:S(2)}) collective-permute-start(f32[2,8,16,512]{3,2,1,0:T(8,128)} %bitcast.34), channel_id=1, source_target_pairs={{0,1},{1,2},{2,3},{3,4},{4,5},{5,6},{6,7},{8,9},{9,10},{10,11},{11... | collective-permute-start | bytes 1572872 | tf_op jit(solution)/shard_map/ppermute | solution.py:243
  10.7 47.5 %copy-start.2 = (bf16[3,16,16,512]{3,2,1,0:T(8,128)(2,1)S(1)}, bf16[3,16,16,512]{3,2,1,0:T(8,128)(2,1)}, u32[]{:S(2)}) copy-start(bf16[3,16,16,512]{3,2,1,0:T(8,128)(2,1)} %scale_ref.1) | copy-start | bytes 2359300
  11.6 43.0 %collective-permute-start.3 = (f32[2,8,16,512]{3,2,1,0:T(8,128)}, f32[2,8,16,512]{3,2,1,0:T(8,128)S(1)}, u32[]{:S(2)}, u32[]{:S(2)}) collective-permute-start(f32[2,8,16,512]{3,2,1,0:T(8,128)} %bitcast.33), channel_id=1, source_target_pairs={{1,0},{2,1},{3,2},{4,3},{5,4},{6,5},{7,6},{9,8},{10,9},{11,10},{12... | collective-permute-start | bytes 1572872 | tf_op jit(solution)/shard_map/ppermute | solution.py:244
  15.8 22.9 %collective-permute-start.1 = (f32[2,8,16,512]{3,2,1,0:T(8,128)}, f32[2,8,16,512]{3,2,1,0:T(8,128)S(1)}, u32[]{:S(2)}, u32[]{:S(2)}) collective-permute-start(f32[2,8,16,512]{3,2,1,0:T(8,128)} %get-tuple-element.20), channel_id=1, source_target_pairs={{8,0},{16,8},{24,16},{9,1},{17,9},{25,17},{10,2},{18,10},{26,18},{... | collective-permute-start | bytes 1572872 | tf_op jit(solution)/shard_map/ppermute | solution.py:240
  17.1 21.6 %collective-permute-start = (f32[2,8,16,512]{3,2,1,0:T(8,128)}, f32[2,8,16,512]{3,2,1,0:T(8,128)S(1)}, u32[]{:S(2)}, u32[]{:S(2)}) collective-permute-start(f32[2,8,16,512]{3,2,1,0:T(8,128)} %get-tuple-element.21), channel_id=1, source_target_pairs={{0,8},{8,16},{16,24},{1,9},{9,17},{17,25},{2,10},{10,18},{18,26},{... | collective-permute-start | bytes 1572872 | tf_op jit(solution)/shard_map/ppermute | solution.py:239
  26.8 0.7 copy-start.4
  30.9 3.4 %copy-start.1 = (bf16[2,4,64,8192]{3,2,1,0:T(8,128)(2,1)S(1)}, bf16[2,4,64,8192]{3,2,1,0:T(8,128)(2,1)}, u32[]{:S(2)}) copy-start(bf16[2,4,64,8192]{3,2,1,0:T(8,128)(2,1)} %matrix_ref.1) | copy-start | bytes 25165828
  39.5 42.1 %all-to-all-start = ((f32[32,1,1152]{2,1,0:T(1,128)}), f32[32,1,1152]{2,1,0:T(1,128)S(1)}, u32[]{:S(2)}, u32[]{:S(2)}) async-start(f32[32,1,1152]{2,1,0:T(1,128)} %reshape.57), calls=%async_computation | async-start | bytes 294912 | tf_op jit(solution)/shard_map/all_to_all | solution.py:277
  49.0 5.6 %collective-permute-start.4 = (f32[2,8,2,512]{3,2,1,0:T(2,128)S(1)}, f32[2,8,2,512]{3,2,1,0:T(2,128)S(1)}, u32[]{:S(2)}, u32[]{:S(2)}) collective-permute-start(f32[2,8,2,512]{3,2,1,0:T(2,128)S(1)} %pad_maximum_fusion.1), channel_id=1, source_target_pairs={{0,1},{1,2},{2,3},{3,4},{4,5},{5,6},{6,7},{8,9},{9,10},{10,11},{11... | collective-permute-start | bytes 196616 | tf_op jit(solution)/shard_map/ppermute | solution.py:252
  52.6 5.6 %collective-permute-start.5 = (f32[2,8,2,512]{3,2,1,0:T(2,128)S(1)}, f32[2,8,2,512]{3,2,1,0:T(2,128)S(1)}, u32[]{:S(2)}, u32[]{:S(2)}) collective-permute-start(f32[2,8,2,512]{3,2,1,0:T(2,128)S(1)} %pad_maximum_fusion.2), channel_id=1, source_target_pairs={{1,0},{2,1},{3,2},{4,3},{5,4},{6,5},{7,6},{9,8},{10,9},{11,10},{12... | collective-permute-start | bytes 196616 | tf_op jit(solution)/shard_map/ppermute | solution.py:253
  58.2 3.4 %copy-start = (f32[2,8,16,16,512]{4,3,2,1,0:T(8,128)S(1)}, f32[2,8,16,16,512]{4,3,2,1,0:T(8,128)}, u32[]{:S(2)}) copy-start(f32[2,8,16,16,512]{4,3,2,1,0:T(8,128)} %volume_ref.1) | copy-start | bytes 25165828
  61.6 20.6 %copy-start.5 = (f32[256,256]{1,0:T(8,128)S(1)}, f32[256,256]{1,0:T(8,128)}, u32[]{:S(2)}) copy-start(f32[256,256]{1,0:T(8,128)} %copy-done.4) | copy-start | bytes 786436

commit v3 on v2

--- a/solution.py
+++ b/solution.py
@@ -76,7 +76,7 @@
         out_specs=pl.BlockSpec((waves, 2 * rows), lambda i: (0, 0)),
         out_shape=jax.ShapeDtypeStruct((waves, 2 * rows), jnp.float32),
         compiler_params=pltpu.CompilerParams(
-            vmem_limit_bytes=40 * 1024 * 1024, dimension_semantics=("arbitrary",)
+            vmem_limit_bytes=56 * 1024 * 1024, dimension_semantics=("arbitrary",)
         ),
         cost_estimate=pl.CostEstimate(
             flops=2 * UMAX * 4 * waves * rows * columns,
@@ -156,15 +156,18 @@
     waves = pl.num_programs(0)
     size_x, size_y, size_z = operated_ref.shape[2:]
     cells = size_x * size_y
-    channel = lax.broadcasted_iota(jnp.int32, (cells, add_ref.shape[1]), 1)
-    lane = lax.broadcasted_iota(jnp.int32, (cells, size_z), 1)
+    channels = add_ref.shape[1]
+    channel = lax.broadcasted_iota(jnp.int32, (channels, size_z), 0)
+    lane = lax.broadcasted_iota(jnp.int32, (channels, size_z), 1)
     for part in range(2):
-        added = jnp.sum(
-            jnp.where(channel == part * waves + wave, add_ref[...], 0.0), axis=1, keepdims=True
+        pick = (channel == part * waves + wave) & (lane == size_z - 1)
+        added = jnp.dot(
+            add_ref[...],
+            pick.astype(jnp.float32),
+            precision=lax.Precision.HIGHEST,
+            preferred_element_type=jnp.float32,
         )
-        own = operated_ref[part, 0].reshape(cells, size_z)
-        total = own + jnp.where(lane == size_z - 1, added, 0.0)
-        out_ref[part, 0] = total.reshape(size_x, size_y, size_z)
+        out_ref[part, 0] = operated_ref[part, 0] + added.reshape(size_x, size_y, size_z)
 
 
 def add_top(operated, cell_add):
@@ -210,7 +213,7 @@
         out_shape=jax.ShapeDtypeStruct(volume.shape, jnp.float32),
         scratch_shapes=[pltpu.VMEM((parts, size_x + 2, size_y, size_z), jnp.float32)],
         compiler_params=pltpu.CompilerParams(
-            vmem_limit_bytes=40 * 1024 * 1024, dimension_semantics=("arbitrary",)
+            vmem_limit_bytes=56 * 1024 * 1024, dimension_semantics=("arbitrary",)
         ),
         cost_estimate=pl.CostEstimate(
             flops=volume.size * 40, bytes_accessed=volume.size * 8, transcendentals=0
@@ -236,12 +239,14 @@
     rows_each = group_rows // n_narrow
 
     up, down = shifts("wide")
-    x_lo = lax.ppermute(volume_field[:, :, -1], "wide", up)
-    x_hi = lax.ppermute(volume_field[:, :, 0], "wide", down)
-
+    x_last, x_first, later = lax.optimization_barrier(
+        (volume_field[:, :, -1], volume_field[:, :, 0], volume_field)
+    )
+    x_lo = lax.ppermute(x_last, "wide", up)
+    x_hi = lax.ppermute(x_first, "wide", down)
     up_y, down_y = shifts("narrow")
-    y_lo = lax.ppermute(volume_field[:, :, :, -1], "narrow", up_y)
-    y_hi = lax.ppermute(volume_field[:, :, :, 0], "narrow", down_y)
+    y_lo = lax.ppermute(later[:, :, :, -1], "narrow", up_y)
+    y_hi = lax.ppermute(later[:, :, :, 0], "narrow", down_y)
 
     partial_rows = bem_partial(density, boundary_matrix, upsample)
     x_lo, x_hi, partial_rows = lax.optimization_barrier((x_lo, x_hi, partial_rows))

time: 90.7 us -> 88.5 us (0.976)
  Pallas kernels: 30.6 us -> 34.7 us
  local copies, waits for them, and re-layouts: 22 us -> 17.9 us
  starting transfers between devices: 26.5 us -> 22.9 us
  other arithmetic: 3.56 us -> 4.67 us
    unnamed x17 -> x15, local copies, waits for them, and re-layouts: 9.17 us -> 0.04 us
    optimization_barrier x0 -> x1, local copies, waits for them, and re-layouts: none -> 8.24 us  [on_device(): lax.optimization_barrier((volume_field[:, :, -1], volume_field[:, :, 0],...]
    slice x1 -> x0, local copies, waits for them, and re-layouts: 4.65 us -> none  [on_device(): y_hi = lax.ppermute(volume_field[:, :, :, 0], 'narrow', down_y)]
    all_to_all x1, starting transfers between devices: 9.25 us -> 6.09 us  [on_device(): lax.all_to_all(outgoing.reshape(devices, 1, -1), BOTH, split_axis=0, conc...]
    pallas_call x1, Pallas kernels: 4.43 us -> 6.63 us  [bem_partial(): pl.pallas_call(functools.partial(bem_kernel, groups=groups, width=width),...]
    another operation x2, other arithmetic: 0.13 us -> 1.37 us  [edges(): return jnp.stack([x_lo[:, :, at], x_hi[:, :, at]], axis=2)]
    pallas_call x1, Pallas kernels: 20 us -> 21.1 us  [stencil(): pl.pallas_call(stencil_kernel, grid=(waves,), in_specs=[whole, face_x, fa...]
    squeeze x1 -> x2, local copies, waits for them, and re-layouts: 2.33 us -> 2.39 us  [the longest x1 2.28 us: on_device(): volume_field[:, :, 0]]
  transfers between devices with their start and end apart: 7 -> 7, of which waited for: 1 -> 1; matrix products, arithmetic and copies ran while one was open for 14% -> 23% of each run, Pallas kernels for 27% -> 32%
where the time goes in v3:
time: 88.5 us; the launch traced here: 87.7 us
  Pallas kernels  34.7 us (39%)
  starting transfers between devices  22.9 us (26%)
  local copies, waits for them, and re-layouts  17.9 us (20%)
  other arithmetic  4.67 us (5%)
  waiting for transfers between devices  3.93 us (4%)
  matrix products  2.16 us (2%)
  between operations  1.54 us (2%)
    pallas_call x1, Pallas kernels, stencil(): pl.pallas_call(stencil_kernel, grid=(waves,), in_specs=[whole, face_x, fa...  21.1 us
    optimization_barrier x1, local copies, waits for them, and re-layouts, on_device(): lax.optimization_barrier((volume_field[:, :, -1], volume_field[:, :, 0],...  8.24 us
    pallas_call x1, Pallas kernels, add_top(): pl.pallas_call(top_kernel, grid=(waves,), in_specs=[block, pl.BlockSpec(c...  6.94 us
    pallas_call x1, Pallas kernels, bem_partial(): pl.pallas_call(functools.partial(bem_kernel, groups=groups, width=width),...  6.63 us
    all_to_all x1, starting transfers between devices, on_device(): lax.all_to_all(outgoing.reshape(devices, 1, -1), BOTH, split_axis=0, conc...  6.09 us
    ppermute x1, starting transfers between devices, on_device(): x_lo = lax.ppermute(x_last, 'wide', up)  4.1 us
    ppermute x1, waiting for transfers between devices, on_device(): edge_hi = lax.ppermute(edges(0), 'narrow', down_y)  3.91 us
    ppermute x1, starting transfers between devices, on_device(): edge_lo = lax.ppermute(edges(size_y - 1), 'narrow', up_y)  3.53 us
  transfers between devices with their start and end apart: 7, of which 1 were waited for; matrix products, arithmetic and copies ran while one was open for 23% of the time, Pallas kernels for 32%

profile of v3, /device:TPU:1, one launch (start us, length us, event | category | flops | bytes accessed | tf_op | source)
XLA Modules:
  0.0 87.7 jit_solution(11826886040006864526)
XLA Ops:
  0.6 2.3 %slice_bitcast_fusion.2 = (f32[2,8,16,512]{3,2,1,0:T(8,128)}, f32[2,8,16,512]{3,2,1,0:T(8,128)}) fusion(f32[2,8,16,16,512]{4,3,2,1,0:T(8,128)} %volume_ref.1), kind=kLoop, calls=%fused_computation.4 | loop fusion | bytes 2097152 | tf_op jit(solution)/shard_map/squeeze | solution.py:243
  2.9 4.1 %collective-permute-start = (f32[2,8,16,512]{3,2,1,0:T(8,128)}, f32[2,8,16,512]{3,2,1,0:T(8,128)S(1)}, u32[]{:S(2)}, u32[]{:S(2)}) collective-permute-start(f32[2,8,16,512]{3,2,1,0:T(8,128)} %get-tuple-element.8), channel_id=1, source_target_pairs={{0,8},{8,16},{16,24},{1,9},{9,17},{17,25},{2,10},{10,18},{18,26},{... | collective-permute-start | bytes 1572872 | tf_op jit(solution)/shard_map/ppermute | solution.py:245
  7.0 1.3 %collective-permute-start.1 = (f32[2,8,16,512]{3,2,1,0:T(8,128)}, f32[2,8,16,512]{3,2,1,0:T(8,128)S(1)}, u32[]{:S(2)}, u32[]{:S(2)}) collective-permute-start(f32[2,8,16,512]{3,2,1,0:T(8,128)} %get-tuple-element.9), channel_id=1, source_target_pairs={{8,0},{16,8},{24,16},{9,1},{17,9},{25,17},{10,2},{18,10},{26,18},{... | collective-permute-start | bytes 1572872 | tf_op jit(solution)/shard_map/ppermute | solution.py:246
  8.3 8.2 %copy.50 = f32[2,8,16,16,512]{4,2,1,0,3:T(8,128)S(1)} copy(f32[2,8,16,16,512]{4,3,2,1,0:T(8,128)} %volume_ref.1) | data formatting | bytes 16777216 | tf_op jit(solution)/shard_map/optimization_barrier | solution.py:242
  16.7 2.9 %collective-permute-start.3 = (f32[2,8,16,512]{3,2,1,0:T(8,128)S(1)}, f32[2,8,16,512]{3,2,1,0:T(8,128)S(1)}, u32[]{:S(2)}, u32[]{:S(2)}) collective-permute-start(f32[2,8,16,512]{3,2,1,0:T(8,128)S(1)} %get-tuple-element.24), channel_id=1, source_target_pairs={{1,0},{2,1},{3,2},{4,3},{5,4},{6,5},{7,6},{9,8},{10,9},{11,10},{12... | collective-permute-start | bytes 1572872 | tf_op jit(solution)/shard_map/ppermute | solution.py:249
  19.6 3.1 %collective-permute-start.2 = (f32[2,8,16,512]{3,2,1,0:T(8,128)S(1)}, f32[2,8,16,512]{3,2,1,0:T(8,128)S(1)}, u32[]{:S(2)}, u32[]{:S(2)}) collective-permute-start(f32[2,8,16,512]{3,2,1,0:T(8,128)S(1)} %get-tuple-element.25), channel_id=1, source_target_pairs={{0,1},{1,2},{2,3},{3,4},{4,5},{5,6},{6,7},{8,9},{9,10},{10,11},{11... | collective-permute-start | bytes 1572872 | tf_op jit(solution)/shard_map/ppermute | solution.py:248
  22.7 2.8 %slice_reduce_fusion = f32[2,8,16,16]{3,2,1,0:T(8,128)S(1)} fusion(f32[2,8,16,16,512]{4,3,2,1,0:T(8,128)} %volume_ref.1), kind=kLoop, calls=%fused_computation | loop fusion | bytes 32768 | tf_op jit(solution)/shard_map/slice | solution.py:273
  26.7 0.9 %fusion = f32[256,256]{1,0:T(8,128)S(1)} fusion(s32[256]{0:T(256)S(1)} %compare_select_fusion, s32[256]{0:T(256)} %bitcast.41), kind=kOutput, calls=%fused_computation.8 | convolution fusion | flops 33685504 | bytes 264192 | tf_op jit(solution)/shard_map/dot_general | solution.py:270
  28.0 0.7 copy.53
  28.7 1.5 %copy.54 = f32[32,128]{1,0:T(8,128)} copy(f32[32,128]{0,1:T(8,128)} %bitcast.38) | data formatting | bytes 32768 | tf_op jit(solution)/shard_map/reshape | solution.py:276
  30.9 1.3 %divide_select_fusion = (f32[4,16]{1,0:T(4,128)}, f32[4,16]{1,0:T(4,128)}) fusion(f32[16]{0:T(128)S(1)} %convert_multiply_fusion, f32[4]{0:T(128)S(1)} %iota_convert_fusion, s32[16]{0:T(128)} %param.12, f32[16]{0:T(128)} %convert_element_type.16), kind=kLoop, calls=%fused_computation.17 | loop fusion | flops 448 | bytes 720 | tf_op jit(solution)/shard_map/jit(_where)/select_n | solution.py:64
  32.2 6.6 %boundary_product.1 = f32[8,128]{1,0:T(8,128)} custom-call(f32[4,16]{1,0:T(4,128)} %get-tuple-element.33.keep_ref, f32[4,16]{1,0:T(4,128)} %get-tuple-element.32.next_ref, f32[2,8,8192]{2,1,0:T(8,128)} %density_ref.1, bf16[2,4,64,8192]{3,2,1,0:T(8,128)(2,1)} %matrix_ref.1), custom_call_target="tpu_custom_call" | custom-call | flops 134217728 | bytes 8912896 | tf_op jit(solution)/shard_map/boundary_product/pallas_call | solution.py:67
  38.9 0.7 pad.clone
  39.6 0.8 reshape.57
  40.4 6.1 %all-to-all-start = ((f32[32,1,1152]{2,1,0:T(1,128)}), f32[32,1,1152]{2,1,0:T(1,128)S(1)}, u32[]{:S(2)}, u32[]{:S(2)}) async-start(f32[32,1,1152]{2,1,0:T(1,128)} %reshape.57), calls=%async_computation | async-start | bytes 294912 | tf_op jit(solution)/shard_map/all_to_all | solution.py:282
  46.6 0.7 pad_maximum_fusion.1
  47.3 3.5 %collective-permute-start.4 = (f32[2,8,2,512]{3,2,1,0:T(2,128)}, f32[2,8,2,512]{3,2,1,0:T(2,128)}, u32[]{:S(2)}, u32[]{:S(2)}) collective-permute-start(f32[2,8,2,512]{3,2,1,0:T(2,128)} %pad_maximum_fusion.1), channel_id=1, source_target_pairs={{0,1},{1,2},{2,3},{3,4},{4,5},{5,6},{6,7},{8,9},{9,10},{10,11},{11... | collective-permute-start | bytes 196616 | tf_op jit(solution)/shard_map/ppermute | solution.py:257
  50.8 0.7 pad_maximum_fusion.2
  51.5 1.9 %collective-permute-start.5 = (f32[2,8,2,512]{3,2,1,0:T(2,128)}, f32[2,8,2,512]{3,2,1,0:T(2,128)}, u32[]{:S(2)}, u32[]{:S(2)}) collective-permute-start(f32[2,8,2,512]{3,2,1,0:T(2,128)} %pad_maximum_fusion.2), channel_id=1, source_target_pairs={{1,0},{2,1},{3,2},{4,3},{5,4},{6,5},{7,6},{9,8},{10,9},{11,10},{12... | collective-permute-start | bytes 196616 | tf_op jit(solution)/shard_map/ppermute | solution.py:258
  53.5 3.9 %collective-permute-done.5.edge_hi = f32[2,8,2,512]{3,2,1,0:T(2,128)} collective-permute-done((f32[2,8,2,512]{3,2,1,0:T(2,128)}, f32[2,8,2,512]{3,2,1,0:T(2,128)}, u32[]{:S(2)}, u32[]{:S(2)}) %collective-permute-start.5) | collective-permute-done | bytes 65568 | tf_op jit(solution)/shard_map/ppermute | solution.py:258
  57.4 21.1 %volume_rows.1.operated_ref = f32[2,8,16,16,512]{4,3,2,1,0:T(8,128)} custom-call(f32[2,8,16,16,512]{4,3,2,1,0:T(8,128)} %volume_ref.1, f32[2,8,16,512]{3,2,1,0:T(8,128)} %copy-done, f32[2,8,16,512]{3,2,1,0:T(8,128)} %copy-done.1, f32[2,8,16,512]{3,2,1,0:T(8,128)} %copy-done.3, f32[2,8,16,512]{3,2,1,0:T(8,128)} %copy-done.2, ...), custom_call_target="tpu_custom_call" | custom-call | flops 83886080 | bytes 16777216 | tf_op jit(solution)/shard_map/volume_rows/pallas_call | solution.py:199
  79.1 1.0 %fusion.7.add_ref = f32[256,16]{1,0:T(8,128)} fusion(f32[256,256]{1,0:T(8,128)S(1)} %fusion, f32[16,256]{1,0:T(8,128)S(1)} %reshape.60), kind=kOutput, calls=%fused_computation.28 | convolution fusion | flops 12582912 | bytes 294912 | tf_op jit(solution)/shard_map/dot_general | solution.py:292
  80.1 0.7 subtract_bitcast_fusion
  80.8 6.9 %slot_rows.1 = f32[2,8,16,16,512]{4,3,2,1,0:T(8,128)} custom-call(f32[2,8,16,16,512]{4,3,2,1,0:T(8,128)} %volume_rows.1.operated_ref, f32[256,16]{1,0:T(8,128)} %fusion.7.add_ref), custom_call_target="tpu_custom_call", output_to_operand_aliasing={{}: (0, {})} | custom-call | flops 2097152 | bytes 4194304 | tf_op jit(solution)/shard_map/slot_rows/pallas_call | solution.py:179
  (39 shorter events, 2.4 us)
Async XLA Ops:
  2.9 23.2 %copy-start.6 = (s32[16]{0:T(128)S(1)}, s32[16]{0:T(128)}, u32[]{:S(2)}) copy-start(s32[16]{0:T(128)} %param.12) | copy-start | bytes 196
  2.9 23.8 %copy-start.5 = (s32[1,1,256]{2,1,0:T(1,128)S(1)}, s32[1,1,256]{2,1,0:T(1,128)}, u32[]{:S(2)}) copy-start(s32[1,1,256]{2,1,0:T(1,128)} %param.14) | copy-start | bytes 3076
  2.9 35.9 %collective-permute-start = (f32[2,8,16,512]{3,2,1,0:T(8,128)}, f32[2,8,16,512]{3,2,1,0:T(8,128)S(1)}, u32[]{:S(2)}, u32[]{:S(2)}) collective-permute-start(f32[2,8,16,512]{3,2,1,0:T(8,128)} %get-tuple-element.8), channel_id=1, source_target_pairs={{0,8},{8,16},{16,24},{1,9},{9,17},{17,25},{2,10},{10,18},{18,26},{... | collective-permute-start | bytes 1572872 | tf_op jit(solution)/shard_map/ppermute | solution.py:245
  7.0 31.8 %collective-permute-start.1 = (f32[2,8,16,512]{3,2,1,0:T(8,128)}, f32[2,8,16,512]{3,2,1,0:T(8,128)S(1)}, u32[]{:S(2)}, u32[]{:S(2)}) collective-permute-start(f32[2,8,16,512]{3,2,1,0:T(8,128)} %get-tuple-element.9), channel_id=1, source_target_pairs={{8,0},{16,8},{24,16},{9,1},{17,9},{25,17},{10,2},{18,10},{26,18},{... | collective-permute-start | bytes 1572872 | tf_op jit(solution)/shard_map/ppermute | solution.py:246
  16.7 36.8 %collective-permute-start.3 = (f32[2,8,16,512]{3,2,1,0:T(8,128)S(1)}, f32[2,8,16,512]{3,2,1,0:T(8,128)S(1)}, u32[]{:S(2)}, u32[]{:S(2)}) collective-permute-start(f32[2,8,16,512]{3,2,1,0:T(8,128)S(1)} %get-tuple-element.24), channel_id=1, source_target_pairs={{1,0},{2,1},{3,2},{4,3},{5,4},{6,5},{7,6},{9,8},{10,9},{11,10},{12... | collective-permute-start | bytes 1572872 | tf_op jit(solution)/shard_map/ppermute | solution.py:249
  19.6 33.9 %collective-permute-start.2 = (f32[2,8,16,512]{3,2,1,0:T(8,128)S(1)}, f32[2,8,16,512]{3,2,1,0:T(8,128)S(1)}, u32[]{:S(2)}, u32[]{:S(2)}) collective-permute-start(f32[2,8,16,512]{3,2,1,0:T(8,128)S(1)} %get-tuple-element.25), channel_id=1, source_target_pairs={{0,1},{1,2},{2,3},{3,4},{4,5},{5,6},{6,7},{8,9},{9,10},{10,11},{11... | collective-permute-start | bytes 1572872 | tf_op jit(solution)/shard_map/ppermute | solution.py:248
  30.2 9.4 %copy-start.4 = (f32[32,128]{1,0:T(8,128)S(1)}, f32[32,128]{1,0:T(8,128)}, u32[]{:S(2)}) copy-start(f32[32,128]{1,0:T(8,128)} %copy.54) | copy-start | bytes 49156
  38.9 18.5 %copy-start = (f32[2,8,16,512]{3,2,1,0:T(8,128)}, f32[2,8,16,512]{3,2,1,0:T(8,128)S(1)}, u32[]{:S(2)}) copy-start(f32[2,8,16,512]{3,2,1,0:T(8,128)S(1)} %collective-permute-done.x_lo) | copy-start | bytes 1572868
  38.9 18.5 %copy-start.1 = (f32[2,8,16,512]{3,2,1,0:T(8,128)}, f32[2,8,16,512]{3,2,1,0:T(8,128)S(1)}, u32[]{:S(2)}) copy-start(f32[2,8,16,512]{3,2,1,0:T(8,128)S(1)} %collective-permute-done.1.x_hi) | copy-start | bytes 1572868
  40.4 38.1 %all-to-all-start = ((f32[32,1,1152]{2,1,0:T(1,128)}), f32[32,1,1152]{2,1,0:T(1,128)S(1)}, u32[]{:S(2)}, u32[]{:S(2)}) async-start(f32[32,1,1152]{2,1,0:T(1,128)} %reshape.57), calls=%async_computation | async-start | bytes 294912 | tf_op jit(solution)/shard_map/all_to_all | solution.py:282
  47.3 6.2 %collective-permute-start.4 = (f32[2,8,2,512]{3,2,1,0:T(2,128)}, f32[2,8,2,512]{3,2,1,0:T(2,128)}, u32[]{:S(2)}, u32[]{:S(2)}) collective-permute-start(f32[2,8,2,512]{3,2,1,0:T(2,128)} %pad_maximum_fusion.1), channel_id=1, source_target_pairs={{0,1},{1,2},{2,3},{3,4},{4,5},{5,6},{6,7},{8,9},{9,10},{10,11},{11... | collective-permute-start | bytes 196616 | tf_op jit(solution)/shard_map/ppermute | solution.py:257
  51.5 5.9 %collective-permute-start.5 = (f32[2,8,2,512]{3,2,1,0:T(2,128)}, f32[2,8,2,512]{3,2,1,0:T(2,128)}, u32[]{:S(2)}, u32[]{:S(2)}) collective-permute-start(f32[2,8,2,512]{3,2,1,0:T(2,128)} %pad_maximum_fusion.2), channel_id=1, source_target_pairs={{1,0},{2,1},{3,2},{4,3},{5,4},{6,5},{7,6},{9,8},{10,9},{11,10},{12... | collective-permute-start | bytes 196616 | tf_op jit(solution)/shard_map/ppermute | solution.py:258
  53.4 4.0 %copy-start.2 = (f32[2,8,16,512]{3,2,1,0:T(8,128)}, f32[2,8,16,512]{3,2,1,0:T(8,128)S(1)}, u32[]{:S(2)}) copy-start(f32[2,8,16,512]{3,2,1,0:T(8,128)S(1)} %collective-permute-done.3.y_hi) | copy-start | bytes 1572868
  53.5 3.9 %copy-start.3 = (f32[2,8,16,512]{3,2,1,0:T(8,128)}, f32[2,8,16,512]{3,2,1,0:T(8,128)S(1)}, u32[]{:S(2)}) copy-start(f32[2,8,16,512]{3,2,1,0:T(8,128)S(1)} %collective-permute-done.2.y_lo) | copy-start | bytes 1572868
